TPU v7x, 256 devices: a whole 4x4x8 slice. The times are simulated.
256 devices in a mesh: gx: 16 (over y, x), gy: 16 (over z, core).
Axes of the slice: x: 4, y: 4, z: 8, core: 2. Of those that a mesh axis runs over, the one named last changes fastest.
Arguments:
- field: float32 [3, 16, 1024, 2048], P(None, None, 'gx', 'gy'), may hold values from -6 to 6
- masks: int32 [2, 7, 32, 64], P(None, None, 'gx', 'gy'), may hold values 0 or 1
Outputs:
- restored: float32 [3, 16, 1024, 2048], P(None, None, 'gx', 'gy')
- coarse: float32 [3, 4, 256, 512], replicated
All inputs are finite; a program needn't handle non-finite values. No bound on the sum of `masks` on one device may be relied on, other than what follows from the above.
Results may differ from a plain program's by a relative error of at most 0.00002.
Values sent between devices are 32-bit elements; how exact they have to be, the bound alone decides.
A program may use at most 128 MiB of HBM per device.

v0:
```python
import jax
import jax.numpy as jnp
from jax import lax
from jax.sharding import PartitionSpec as P

BLOCK = 32


def extended(x, sides, width):
    for axis, dim in sides:
        count, length = (lax.axis_size(axis), x.shape[dim])
        up = [(i, (i + 1) % count) for i in range(count)]
        down = [(j, i) for i, j in up]
        last = lax.slice_in_dim(x, length - width, length, axis=dim)
        leading = lax.slice_in_dim(x, 0, width, axis=dim)
        before = lax.ppermute(last, axis, up)
        after = lax.ppermute(leading, axis, down)
        x = jnp.concatenate([before, x, after], axis=dim)
    return x


def laid_out(tiles, dim):
    lengths = list(tiles.shape[1:])
    lengths[dim] *= tiles.shape[0]
    return jnp.moveaxis(tiles, 0, dim).reshape(lengths)


def from_everyone(x, axis):
    count = lax.axis_size(axis)
    return lax.all_to_all(jnp.broadcast_to(x[None], (count, *x.shape)), axis, 0, 0, tiled=True)


def gathered_copies(x, axis, dim):
    return laid_out(from_everyone(x, axis), dim)


def take_slice(volume, start, stop, stride, direction):
    return lax.slice_in_dim(volume, start, stop, stride, direction)


def lift_forward(padded, direction):
    length = padded.shape[direction] - 4
    even_cells = take_slice(padded, 2, length + 2, 2, direction)
    odd_cells = take_slice(padded, 3, length + 3, 2, direction)
    next_even = take_slice(padded, 4, length + 4, 2, direction)
    detail = odd_cells - 0.5 * (even_cells + next_even)
    first_detail = take_slice(padded, 1, 2, 1, direction) - 0.5 * (
        take_slice(padded, 0, 1, 1, direction) + take_slice(padded, 2, 3, 1, direction)
    )
    previous = jnp.concatenate(
        [first_detail, take_slice(detail, 0, length // 2 - 1, 1, direction)], direction
    )
    smooth = even_cells + 0.25 * (previous + detail)
    return jnp.concatenate([smooth, detail], 0)


def lift_inverse(padded, direction):
    middle = padded.shape[0] // 2
    smooth_pad = padded[:middle]
    detail_pad = padded[middle:]
    length = padded.shape[direction] - 2
    even_ext = take_slice(smooth_pad, 1, length + 2, 1, direction) - 0.25 * (
        take_slice(detail_pad, 0, length + 1, 1, direction)
        + take_slice(detail_pad, 1, length + 2, 1, direction)
    )
    even_cells = take_slice(even_ext, 0, length, 1, direction)
    next_even = take_slice(even_ext, 1, length + 1, 1, direction)
    odd_cells = take_slice(detail_pad, 1, length + 1, 1, direction) + 0.5 * (even_cells + next_even)
    target_shape = list(even_cells.shape)
    target_shape[direction] = 2 * length
    return jnp.stack([even_cells, odd_cells], direction + 1).reshape(target_shape)


def mirror_forward(volume, direction):
    length = volume.shape[direction]
    return jnp.concatenate(
        [
            take_slice(volume, 2, 3, 1, direction),
            take_slice(volume, 1, 2, 1, direction),
            volume,
            take_slice(volume, length - 2, length - 1, 1, direction),
            take_slice(volume, length - 3, length - 2, 1, direction),
        ],
        direction,
    )


def mirror_inverse(volume, direction):
    middle = volume.shape[0] // 2
    length = volume.shape[direction]
    smooth = volume[:middle]
    detail = volume[middle:]
    smooth_pad = jnp.concatenate(
        [
            take_slice(smooth, 0, 1, 1, direction),
            smooth,
            take_slice(smooth, length - 1, length, 1, direction),
        ],
        direction,
    )
    detail_pad = jnp.concatenate(
        [
            take_slice(detail, 0, 1, 1, direction),
            detail,
            take_slice(detail, length - 2, length - 1, 1, direction),
        ],
        direction,
    )
    return jnp.concatenate([smooth_pad, detail_pad], 0)


def expand_mask(mask_block, block_width):
    return jnp.repeat(jnp.repeat(mask_block, block_width, 1), block_width, 2).astype(jnp.float32)


def grid_forward(volume):
    padded = extended(volume, (("gx", 3), ("gy", 4)), 2)
    volume = lift_forward(padded, 3)
    volume = lift_forward(volume, 4)
    return lift_forward(mirror_forward(volume, 2), 2)


def grid_inverse(volume):
    volume = lift_inverse(mirror_inverse(volume, 2), 2)
    padded = extended(volume, (("gx", 3), ("gy", 4)), 1)
    volume = lift_inverse(padded, 4)
    volume = lift_inverse(volume, 3)
    return volume


def gather_coarse(local_coarse):
    partial_rows = gathered_copies(local_coarse, "gy", 3)
    return lax.all_gather(partial_rows, "gx", axis=2, tiled=True)


def body(field, masks):
    coarse = None
    local_coarse = None
    volume = field[None]
    detail_list = []
    volume = grid_forward(volume)
    detail_list.append(volume[1:] * expand_mask(masks[0], BLOCK >> 1)[:, None, None, :, :])
    volume = volume[:1]
    level_index = 1
    volume = grid_forward(volume)
    kept_mask = expand_mask(masks[level_index], BLOCK >> level_index + 1)
    detail_list.append(volume[1:] * kept_mask[:, None, None, :, :])
    volume = volume[:1]
    local_coarse = volume[0]
    level_index = 1
    volume = grid_inverse(jnp.concatenate([volume, detail_list[level_index]], 0))
    volume = grid_inverse(jnp.concatenate([volume, detail_list[0]], 0))
    restored = volume[0]
    coarse = gather_coarse(local_coarse)
    return (restored, coarse)


def solution(mesh):
    placed = (P(None, None, "gx", "gy"), P(None, None, "gx", "gy"))
    return jax.shard_map(
        body,
        mesh=mesh,
        in_specs=placed,
        out_specs=(P(None, None, "gx", "gy"), P()),
        check_vma=False,
    )
```

profile of v0, /device:TPU:1, one launch (start us, length us, event | category | flops | bytes accessed | tf_op | source)
XLA Modules:
  0.0 345.0 jit_solution(10423994008868034002)
XLA Ops:
  7.2 1.1 fusion.90
  8.3 2.1 collective-permute-start
  10.4 3.8 %collective-permute-start.1 = (f32[1,3,16,2,128]{4,3,2,1,0:T(2,128)S(1)}, f32[1,3,16,2,128]{4,3,2,1,0:T(2,128)S(1)}, u32[]{:S(2)}, u32[]{:S(2)}) collective-permute-start(f32[1,3,16,2,128]{4,3,2,1,0:T(2,128)S(1)} %get-tuple-element.35), channel_id=1, source_target_pairs={{16,0},{32,16},{48,32},{64,48},{80,64},{96,80},{112,96},{128,112},... | collective-permute-start | bytes 147464 | tf_op jit(solution)/shard_map/ppermute | solution.py:17
  14.2 1.4 collective-permute-done
  16.8 1.6 pad_maximum_fusion.12
  19.0 1.3 copy.109
  20.2 3.2 collective-permute-start.2
  24.9 1.9 copy.111
  26.8 1.1 collective-permute-done.3
  27.9 1.9 copy.112
  29.7 4.2 %pad_maximum_fusion.5 = f32[1,3,16,68,132]{4,3,2,1,0:T(8,128)S(1)} fusion(f32[1,3,16,68,2]{4,3,2,1,0:T(8,128)} %copy.112, f32[1,3,16,2,128]{4,3,2,1,0:T(2,128)} %copy-done.24, f32[1,3,16,64,128]{4,3,2,1,0:T(8,128)} %bitcast.73, f32[1,3,16,2,128]{4,3,2,1,0:T(2,128)} %copy-done.23, f32[1,3,16,68,2]{4,3,2,1,0:T(8,128)} %copy.111), kind=kLoop, calls=%fused_computation.23 | loop fusion | flops 1723392 | bytes 3446784 | tf_op jit(solution)/shard_map/concatenate | solution.py:18
  33.9 4.6 %slice.382 = f32[1,3,16,32,132]{4,3,2,1,0:T(8,128)} slice(f32[1,3,16,68,132]{4,3,2,1,0:T(8,128)S(1)} %pad_maximum_fusion.5), slice={[0:1:1], [0:3:1], [0:16:1], [2:66:2], [0:132:1]} | slice | bytes 1622016 | tf_op jit(solution)/shard_map/slice | solution.py:38
  38.5 4.4 %slice.386 = f32[1,3,16,32,132]{4,3,2,1,0:T(8,128)} slice(f32[1,3,16,68,132]{4,3,2,1,0:T(8,128)S(1)} %pad_maximum_fusion.5), slice={[0:1:1], [0:3:1], [0:16:1], [3:67:2], [0:132:1]} | slice | bytes 1622016 | tf_op jit(solution)/shard_map/slice | solution.py:38
  42.9 4.4 %slice.387 = f32[1,3,16,32,132]{4,3,2,1,0:T(8,128)} slice(f32[1,3,16,68,132]{4,3,2,1,0:T(8,128)S(1)} %pad_maximum_fusion.5), slice={[0:1:1], [0:3:1], [0:16:1], [4:68:2], [0:132:1]} | slice | bytes 1622016 | tf_op jit(solution)/shard_map/slice | solution.py:38
  47.3 3.0 multiply_subtract_fusion.2
  51.0 2.0 fusion.17
  53.4 36.9 %slice.389 = f32[2,3,16,32,64]{4,3,2,1,0:T(8,128)} slice(f32[2,3,16,32,132]{4,3,2,1,0:T(8,128)S(1)} %pad_maximum_fusion.2), slice={[0:2:1], [0:3:1], [0:16:1], [0:32:1], [2:130:2]} | slice | bytes 1572864 | tf_op jit(solution)/shard_map/slice | solution.py:38
  90.2 36.9 %slice.393 = f32[2,3,16,32,64]{4,3,2,1,0:T(8,128)} slice(f32[2,3,16,32,132]{4,3,2,1,0:T(8,128)S(1)} %pad_maximum_fusion.2), slice={[0:2:1], [0:3:1], [0:16:1], [0:32:1], [3:131:2]} | slice | bytes 1572864 | tf_op jit(solution)/shard_map/slice | solution.py:38
  127.1 36.8 %slice.394 = f32[2,3,16,32,64]{4,3,2,1,0:T(8,128)} slice(f32[2,3,16,32,132]{4,3,2,1,0:T(8,128)S(1)} %pad_maximum_fusion.2), slice={[0:2:1], [0:3:1], [0:16:1], [0:32:1], [4:132:2]} | slice | bytes 1572864 | tf_op jit(solution)/shard_map/slice | solution.py:38
  163.9 3.1 multiply_subtract_fusion.1
  170.7 5.0 %collective-permute-start.5 = (f32[1,3,8,2,64]{4,3,2,1,0:T(2,128)S(1)}, f32[1,3,8,2,64]{4,3,2,1,0:T(2,128)S(1)}, u32[]{:S(2)}, u32[]{:S(2)}) collective-permute-start(f32[1,3,8,2,64]{4,3,2,1,0:T(2,128)S(1)} %get-tuple-element.33), channel_id=1, source_target_pairs={{16,0},{32,16},{48,32},{64,48},{80,64},{96,80},{112,96},{128,112},... | collective-permute-start | bytes 36872 | tf_op jit(solution)/shard_map/ppermute | solution.py:17
  177.0 2.3 collective-permute-start.6
  179.3 1.4 collective-permute-start.7
  180.8 4.3 %collective-permute-done.6 = f32[1,3,8,36,2]{4,3,2,1,0:T(8,128)S(1)} collective-permute-done((f32[1,3,8,36,2]{4,3,2,1,0:T(8,128)S(1)}, f32[1,3,8,36,2]{4,3,2,1,0:T(8,128)S(1)}, u32[]{:S(2)}, u32[]{:S(2)}) %collective-permute-start.6) | collective-permute-done | bytes 6944 | tf_op jit(solution)/shard_map/ppermute | solution.py:16
  185.1 2.8 collective-permute-done.7
  189.1 3.8 %slice.417 = f32[2,3,8,16,32]{4,3,2,1,0:T(8,128)S(1)} slice(f32[2,3,8,16,68]{4,3,2,1,0:T(8,128)S(1)} %pad_maximum_fusion.19), slice={[0:2:1], [0:3:1], [0:8:1], [0:16:1], [2:66:2]} | slice | bytes 196608 | tf_op jit(solution)/shard_map/slice | solution.py:38
  192.9 3.8 %slice.421 = f32[2,3,8,16,32]{4,3,2,1,0:T(8,128)S(1)} slice(f32[2,3,8,16,68]{4,3,2,1,0:T(8,128)S(1)} %pad_maximum_fusion.19), slice={[0:2:1], [0:3:1], [0:8:1], [0:16:1], [3:67:2]} | slice | bytes 196608 | tf_op jit(solution)/shard_map/slice | solution.py:38
  196.7 3.8 %slice.422 = f32[2,3,8,16,32]{4,3,2,1,0:T(8,128)S(1)} slice(f32[2,3,8,16,68]{4,3,2,1,0:T(8,128)S(1)} %pad_maximum_fusion.19), slice={[0:2:1], [0:3:1], [0:8:1], [0:16:1], [4:68:2]} | slice | bytes 196608 | tf_op jit(solution)/shard_map/slice | solution.py:38
  203.0 23.7 %all_to_all.5 = f32[16,1,6144]{2,1,0:T(1,128)S(1)} all-to-all(f32[16,1,6144]{2,1,0:T(1,128)S(1)} %reshape.46), channel_id=1, replica_groups=mesh['gx'=16,'gy'=16] {'gy'}, dimensions={0} | all-to-all | bytes 786432 | tf_op jit(solution)/shard_map/all_to_all | solution.py:30
  227.2 1.5 reduce
  230.2 1.4 reshape.45
  233.7 5.7 %collective-permute-start.9 = (f32[4,3,8,1,32]{4,3,2,1,0:T(1,128)S(1)}, f32[4,3,8,1,32]{4,3,2,1,0:T(1,128)S(1)}, u32[]{:S(2)}, u32[]{:S(2)}) collective-permute-start(f32[4,3,8,1,32]{4,3,2,1,0:T(1,128)S(1)} %get-tuple-element.43), channel_id=1, source_target_pairs={{16,0},{32,16},{48,32},{64,48},{80,64},{96,80},{112,96},{128,112},... | collective-permute-start | bytes 36872 | tf_op jit(solution)/shard_map/ppermute | solution.py:17
  241.0 1.8 fusion.91
  242.8 2.5 copy.116
  245.4 2.5 copy.118
  248.0 1.7 collective-permute-start.11
  250.4 2.5 copy.117
  252.9 2.5 copy.119
  255.4 1.8 pad_maximum_fusion.16
  258.7 1.1 fusion.37
  259.9 1.5 copy.123
  261.4 2.3 copy.122
  263.7 1.6 fusion.35
  265.8 1.2 pad_maximum_fusion.13
  267.0 1.9 copy.124
  271.8 5.3 %collective-permute-start.13 = (f32[4,3,16,1,64]{4,3,2,1,0:T(1,128)S(1)}, f32[4,3,16,1,64]{4,3,2,1,0:T(1,128)S(1)}, u32[]{:S(2)}, u32[]{:S(2)}) collective-permute-start(f32[4,3,16,1,64]{4,3,2,1,0:T(1,128)S(1)} %get-tuple-element.17), channel_id=1, source_target_pairs={{16,0},{32,16},{48,32},{64,48},{80,64},{96,80},{112,96},{128,112},... | collective-permute-start | bytes 147464 | tf_op jit(solution)/shard_map/ppermute | solution.py:17
  277.2 5.2 %collective-permute-done.12 = f32[4,3,16,1,64]{4,3,2,1,0:T(1,128)S(1)} collective-permute-done((f32[4,3,16,1,64]{4,3,2,1,0:T(1,128)S(1)}, f32[4,3,16,1,64]{4,3,2,1,0:T(1,128)S(1)}, u32[]{:S(2)}, u32[]{:S(2)}) %collective-permute-start.12) | collective-permute-done | bytes 49184 | tf_op jit(solution)/shard_map/ppermute | solution.py:16
  283.1 4.6 %fusion.84 = (f32[4,3,16,34,1]{4,3,2,1,0:T(8,128)}, f32[4,3,16,34,1]{4,3,2,1,0:T(8,128)}) fusion(f32[4,3,16,34,64]{4,3,2,1,0:T(8,128)S(1)} %pad_maximum_fusion.3), kind=kLoop, calls=%fused_computation.197 | loop fusion | bytes 104448 | tf_op jit(solution)/shard_map/slice | solution.py:14
  287.7 3.3 copy.128
  292.0 3.7 %copy.130 = f32[4,3,16,34,1]{3,2,4,1,0:T(8,128)} copy(f32[4,3,16,34,1]{4,3,2,1,0:T(8,128)} %get-tuple-element.12) | data formatting | bytes 52224 | tf_op jit(solution)/shard_map/slice | solution.py:14
  296.5 2.9 copy.129
  299.3 3.7 %copy.131 = f32[4,3,16,34,1]{4,3,2,1,0:T(8,128)} copy(f32[4,3,16,34,1]{3,2,4,1,0:T(8,128)} %collective-permute-done.15) | data formatting | bytes 52224 | tf_op jit(solution)/shard_map/ppermute | solution.py:16
  303.0 3.4 pad_maximum_fusion.4
  306.5 1.0 fusion.11
  307.5 1.1 copy-done.1
  309.2 1.8 fusion.6
  311.0 2.6 copy.134
  313.5 2.9 copy.135
  316.5 3.6 %fusion.4 = f32[1,3,16,33,128]{3,2,4,1,0:T(8,128)S(1)} fusion(f32[1,3,16,34,128]{3,2,4,1,0:T(8,128)S(1)} %bitcast.60, f32[1,3,16,34,128]{3,2,4,1,0:T(8,128)} %bitcast.68), kind=kLoop, calls=%fused_computation.30 | loop fusion | flops 608256 | bytes 3244032 | tf_op jit(solution)/shard_map/sub | solution.py:62
  320.1 1.7 slice_bitcast_fusion
  321.7 3.3 pad_maximum_fusion
  325.1 5.1 %copy.136 = f32[1,3,16,32,2,128]{5,2,4,3,1,0:T(8,128)S(1)} copy(f32[1,3,16,32,2,128]{3,2,5,1,4,0:T(8,128)} %pad_maximum_fusion) | data formatting | bytes 3145728 | tf_op jit(solution)/shard_map/stack | solution.py:71
  330.2 1.6 copy.138
  331.8 6.2 %copy.150 = f32[3,4,256,512]{3,2,1,0:T(8,128)} copy(f32[3,4,256,512]{3,2,1,0:T(8,128)} %all-gather.2.cloned.1.call-done) | data formatting | bytes 12582912
  (147 shorter events, 27.3 us)
Async XLA Ops:
  7.2 324.6 %all-gather.2.cloned.1.call-start = ((), (), s32[]{:S(2)}) async-start(), calls=%async_computation.1 | async-start | bytes 6684672 | tf_op jit(solution)/shard_map/all_gather | solution.py:133
  8.3 7.3 %collective-permute-start = (f32[1,3,16,2,128]{4,3,2,1,0:T(2,128)S(1)}, f32[1,3,16,2,128]{4,3,2,1,0:T(2,128)S(1)}, u32[]{:S(2)}, u32[]{:S(2)}) collective-permute-start(f32[1,3,16,2,128]{4,3,2,1,0:T(2,128)S(1)} %get-tuple-element.34), channel_id=1, source_target_pairs={{0,16},{16,32},{32,48},{48,64},{64,80},{80,96},{96,112},{112,128},... | collective-permute-start | bytes 147464 | tf_op jit(solution)/shard_map/ppermute | solution.py:16
  10.4 5.2 %collective-permute-start.1 = (f32[1,3,16,2,128]{4,3,2,1,0:T(2,128)S(1)}, f32[1,3,16,2,128]{4,3,2,1,0:T(2,128)S(1)}, u32[]{:S(2)}, u32[]{:S(2)}) collective-permute-start(f32[1,3,16,2,128]{4,3,2,1,0:T(2,128)S(1)} %get-tuple-element.35), channel_id=1, source_target_pairs={{16,0},{32,16},{48,32},{64,48},{80,64},{96,80},{112,96},{128,112},... | collective-permute-start | bytes 147464 | tf_op jit(solution)/shard_map/ppermute | solution.py:17
  15.6 0.6 copy-start.23
  16.2 0.6 copy-start.24
  20.2 4.7 %collective-permute-start.2 = (f32[1,3,16,68,2]{3,2,4,1,0:T(8,128)}, f32[1,3,16,68,2]{3,2,4,1,0:T(8,128)S(1)}, u32[]{:S(2)}, u32[]{:S(2)}) collective-permute-start(f32[1,3,16,68,2]{3,2,4,1,0:T(8,128)} %copy.109), channel_id=1, source_target_pairs={{0,1},{1,2},{2,3},{3,4},{4,5},{5,6},{6,7},{7,8},{8,9},{9,10},{10,1... | collective-permute-start | bytes 78344 | tf_op jit(solution)/shard_map/ppermute | solution.py:16
  24.0 3.8 %collective-permute-start.3 = (f32[1,3,16,68,2]{3,2,4,1,0:T(8,128)S(1)}, f32[1,3,16,68,2]{3,2,4,1,0:T(8,128)S(1)}, u32[]{:S(2)}, u32[]{:S(2)}) collective-permute-start(f32[1,3,16,68,2]{3,2,4,1,0:T(8,128)S(1)} %copy.110), channel_id=1, source_target_pairs={{1,0},{2,1},{3,2},{4,3},{5,4},{6,5},{7,6},{8,7},{9,8},{10,9},{11,1... | collective-permute-start | bytes 78344 | tf_op jit(solution)/shard_map/ppermute | solution.py:17
  47.3 3.0 copy-start.7
  163.9 3.1 copy-start.8
  163.9 3.3 copy-start.11
  169.5 1.1 copy-start.2
  170.6 6.4 %copy-start.9 = (f32[4,3,8,32,64]{4,3,2,1,0:T(8,128)}, f32[4,3,8,32,64]{4,3,2,1,0:T(8,128)S(1)}, u32[]{:S(2)}) copy-start(f32[4,3,8,32,64]{4,3,2,1,0:T(8,128)S(1)} %fusion.30) | copy-start | bytes 2359300
  170.6 6.1 %collective-permute-start.4 = (f32[1,3,8,2,64]{4,3,2,1,0:T(2,128)S(1)}, f32[1,3,8,2,64]{4,3,2,1,0:T(2,128)S(1)}, u32[]{:S(2)}, u32[]{:S(2)}) collective-permute-start(f32[1,3,8,2,64]{4,3,2,1,0:T(2,128)S(1)} %get-tuple-element.32), channel_id=1, source_target_pairs={{0,16},{16,32},{32,48},{48,64},{64,80},{80,96},{96,112},{112,128},... | collective-permute-start | bytes 36872 | tf_op jit(solution)/shard_map/ppermute | solution.py:16
  170.7 6.0 %collective-permute-start.5 = (f32[1,3,8,2,64]{4,3,2,1,0:T(2,128)S(1)}, f32[1,3,8,2,64]{4,3,2,1,0:T(2,128)S(1)}, u32[]{:S(2)}, u32[]{:S(2)}) collective-permute-start(f32[1,3,8,2,64]{4,3,2,1,0:T(2,128)S(1)} %get-tuple-element.33), channel_id=1, source_target_pairs={{16,0},{32,16},{48,32},{64,48},{80,64},{96,80},{112,96},{128,112},... | collective-permute-start | bytes 36872 | tf_op jit(solution)/shard_map/ppermute | solution.py:17
  177.0 8.1 %collective-permute-start.6 = (f32[1,3,8,36,2]{4,3,2,1,0:T(8,128)S(1)}, f32[1,3,8,36,2]{4,3,2,1,0:T(8,128)S(1)}, u32[]{:S(2)}, u32[]{:S(2)}) collective-permute-start(f32[1,3,8,36,2]{4,3,2,1,0:T(8,128)S(1)} %get-tuple-element.56), channel_id=1, source_target_pairs={{0,1},{1,2},{2,3},{3,4},{4,5},{5,6},{6,7},{7,8},{8,9},{9,10},{10,1... | collective-permute-start | bytes 20744 | tf_op jit(solution)/shard_map/ppermute | solution.py:16
  179.3 8.6 %collective-permute-start.7 = (f32[1,3,8,36,2]{4,3,2,1,0:T(8,128)S(1)}, f32[1,3,8,36,2]{4,3,2,1,0:T(8,128)S(1)}, u32[]{:S(2)}, u32[]{:S(2)}) collective-permute-start(f32[1,3,8,36,2]{4,3,2,1,0:T(8,128)S(1)} %get-tuple-element.57), channel_id=1, source_target_pairs={{1,0},{2,1},{3,2},{4,3},{5,4},{6,5},{7,6},{8,7},{9,8},{10,9},{11,1... | collective-permute-start | bytes 20744 | tf_op jit(solution)/shard_map/ppermute | solution.py:17
  201.3 0.8 copy-start.13
  230.1 1.4 copy-start.25
  230.1 2.9 copy-start.14
  231.5 1.7 copy-start.15
  233.4 6.1 %copy-start.3 = (f32[4,3,8,32,64]{4,3,2,1,0:T(8,128)S(1)}, f32[4,3,8,32,64]{4,3,2,1,0:T(8,128)}, u32[]{:S(2)}) copy-start(f32[4,3,8,32,64]{4,3,2,1,0:T(8,128)} %copy-done.2) | copy-start | bytes 2359300
  233.4 6.1 %copy-start.10 = (f32[4,3,8,32,64]{4,3,2,1,0:T(8,128)S(1)}, f32[4,3,8,32,64]{4,3,2,1,0:T(8,128)}, u32[]{:S(2)}) copy-start(f32[4,3,8,32,64]{4,3,2,1,0:T(8,128)} %copy-done.9) | copy-start | bytes 2359300
  233.4 6.1 %copy-start.18 = (f32[7,32,64]{2,1,0:T(8,128)S(1)}, f32[7,32,64]{2,1,0:T(8,128)}, u32[]{:S(2)}) copy-start(f32[7,32,64]{2,1,0:T(8,128)} %copy.126) | copy-start | bytes 172036
  233.7 6.8 %collective-permute-start.8 = (f32[4,3,8,1,32]{4,3,2,1,0:T(1,128)S(1)}, f32[4,3,8,1,32]{4,3,2,1,0:T(1,128)S(1)}, u32[]{:S(2)}, u32[]{:S(2)}) collective-permute-start(f32[4,3,8,1,32]{4,3,2,1,0:T(1,128)S(1)} %get-tuple-element.42), channel_id=1, source_target_pairs={{0,16},{16,32},{32,48},{48,64},{64,80},{80,96},{96,112},{112,128},... | collective-permute-start | bytes 36872 | tf_op jit(solution)/shard_map/ppermute | solution.py:16
  233.7 7.0 %collective-permute-start.9 = (f32[4,3,8,1,32]{4,3,2,1,0:T(1,128)S(1)}, f32[4,3,8,1,32]{4,3,2,1,0:T(1,128)S(1)}, u32[]{:S(2)}, u32[]{:S(2)}) collective-permute-start(f32[4,3,8,1,32]{4,3,2,1,0:T(1,128)S(1)} %get-tuple-element.43), channel_id=1, source_target_pairs={{16,0},{32,16},{48,32},{64,48},{80,64},{96,80},{112,96},{128,112},... | collective-permute-start | bytes 36872 | tf_op jit(solution)/shard_map/ppermute | solution.py:17
  240.5 2.3 copy-start.19
  240.7 2.1 copy-start.21
  241.0 1.8 copy-start.5
  245.3 5.1 %collective-permute-start.10 = (f32[4,3,8,18,1]{3,2,4,1,0:T(8,128)}, f32[4,3,8,18,1]{3,2,4,1,0:T(8,128)}, u32[]{:S(2)}, u32[]{:S(2)}) collective-permute-start(f32[4,3,8,18,1]{3,2,4,1,0:T(8,128)} %copy.116), channel_id=1, source_target_pairs={{1,0},{2,1},{3,2},{4,3},{5,4},{6,5},{7,6},{8,7},{9,8},{10,9},{11,1... | collective-permute-start | bytes 20744 | tf_op jit(solution)/shard_map/ppermute | solution.py:17
  248.0 4.9 %collective-permute-start.11 = (f32[4,3,8,18,1]{3,2,4,1,0:T(8,128)}, f32[4,3,8,18,1]{3,2,4,1,0:T(8,128)}, u32[]{:S(2)}, u32[]{:S(2)}) collective-permute-start(f32[4,3,8,18,1]{3,2,4,1,0:T(8,128)} %copy.118), channel_id=1, source_target_pairs={{0,1},{1,2},{2,3},{3,4},{4,5},{5,6},{6,7},{7,8},{8,9},{9,10},{10,1... | collective-permute-start | bytes 20744 | tf_op jit(solution)/shard_map/ppermute | solution.py:16
  255.4 1.8 copy-start.12
  255.4 1.8 copy-start.20
  255.4 1.8 copy-start.22
  257.2 1.3 copy-start.6
  268.9 0.9 copy-start.16
  268.9 1.0 copy-start.17
  271.8 10.6 %collective-permute-start.12 = (f32[4,3,16,1,64]{4,3,2,1,0:T(1,128)S(1)}, f32[4,3,16,1,64]{4,3,2,1,0:T(1,128)S(1)}, u32[]{:S(2)}, u32[]{:S(2)}) collective-permute-start(f32[4,3,16,1,64]{4,3,2,1,0:T(1,128)S(1)} %get-tuple-element.16), channel_id=1, source_target_pairs={{0,16},{16,32},{32,48},{48,64},{64,80},{80,96},{96,112},{112,128},... | collective-permute-start | bytes 147464 | tf_op jit(solution)/shard_map/ppermute | solution.py:16
  271.8 10.5 %collective-permute-start.13 = (f32[4,3,16,1,64]{4,3,2,1,0:T(1,128)S(1)}, f32[4,3,16,1,64]{4,3,2,1,0:T(1,128)S(1)}, u32[]{:S(2)}, u32[]{:S(2)}) collective-permute-start(f32[4,3,16,1,64]{4,3,2,1,0:T(1,128)S(1)} %get-tuple-element.17), channel_id=1, source_target_pairs={{16,0},{32,16},{48,32},{64,48},{80,64},{96,80},{112,96},{128,112},... | collective-permute-start | bytes 147464 | tf_op jit(solution)/shard_map/ppermute | solution.py:17
  283.1 4.6 %copy-start = (f32[4,3,16,34,64]{4,3,2,1,0:T(8,128)}, f32[4,3,16,34,64]{4,3,2,1,0:T(8,128)S(1)}, u32[]{:S(2)}) copy-start(f32[4,3,16,34,64]{4,3,2,1,0:T(8,128)S(1)} %pad_maximum_fusion.3) | copy-start | bytes 5013508
  291.0 5.5 %collective-permute-start.14 = (f32[4,3,16,34,1]{3,2,4,1,0:T(8,128)S(1)}, f32[4,3,16,34,1]{3,2,4,1,0:T(8,128)S(1)}, u32[]{:S(2)}, u32[]{:S(2)}) collective-permute-start(f32[4,3,16,34,1]{3,2,4,1,0:T(8,128)S(1)} %copy.128), channel_id=1, source_target_pairs={{1,0},{2,1},{3,2},{4,3},{5,4},{6,5},{7,6},{8,7},{9,8},{10,9},{11,1... | collective-permute-start | bytes 78344 | tf_op jit(solution)/shard_map/ppermute | solution.py:17
  295.7 3.7 %collective-permute-start.15 = (f32[4,3,16,34,1]{3,2,4,1,0:T(8,128)}, f32[4,3,16,34,1]{3,2,4,1,0:T(8,128)}, u32[]{:S(2)}, u32[]{:S(2)}) collective-permute-start(f32[4,3,16,34,1]{3,2,4,1,0:T(8,128)} %copy.130), channel_id=1, source_target_pairs={{0,1},{1,2},{2,3},{3,4},{4,5},{5,6},{6,7},{7,8},{8,9},{9,10},{10,1... | collective-permute-start | bytes 78344 | tf_op jit(solution)/shard_map/ppermute | solution.py:16
  303.0 3.5 %copy-start.4 = (f32[4,3,16,34,1]{4,3,2,1,0:T(8,128)S(1)}, f32[4,3,16,34,1]{4,3,2,1,0:T(8,128)}, u32[]{:S(2)}) copy-start(f32[4,3,16,34,1]{4,3,2,1,0:T(8,128)} %copy.131) | copy-start | bytes 78340
  306.4 2.1 copy-start.1
Sparse Core Ops, SparseCore 0:
  231.7 65.0 all-gather.1
where the time goes:
time: 351 us; the launch traced here: 345 us
  local copies, waits for them, and re-layouts  210 us (60%)
  other arithmetic  46.4 us (13%)
  starting transfers between devices  33 us (9%)
  blocking collectives  23.7 us (7%)
  waiting for transfers between devices  17.3 us (5%)
  between operations  15 us (4%)
    slice x16, local copies, waits for them, and re-layouts, take_slice(): return lax.slice_in_dim(volume, start, stop, stride, direction)  137 us
    all_to_all x1, blocking collectives, from_everyone(): lax.all_to_all(jnp.broadcast_to(x[None], (count, *x.shape)), axis, 0, 0,...  23.7 us
    ppermute x8, starting transfers between devices, extended(): after = lax.ppermute(leading, axis, down)  22.6 us
    slice x11, local copies, waits for them, and re-layouts, extended(): last = lax.slice_in_dim(x, length - width, length, axis=dim)  15.9 us
    unnamed x56, local copies, waits for them, and re-layouts  13.5 us
    ppermute x8, waiting for transfers between devices, extended(): before = lax.ppermute(last, axis, up)  13.1 us
    concatenate x8, other arithmetic, extended(): x = jnp.concatenate([before, x, after], axis=dim)  12.4 us
    another operation x12, other arithmetic, lift_inverse(): jnp.stack([even_cells, odd_cells], direction + 1).reshape(target_shape)  11.5 us
  transfers between devices with their start and end apart: 17, of which 9 were waited for; matrix products, arithmetic and copies ran while one was open for 23% of the time, Pallas kernels for 0%

commit v1 on v0

v1 whole, which is shorter than its diff:
```python
import jax
import jax.numpy as jnp
import numpy as np
from jax import lax
from jax.experimental import pallas as pl
from jax.experimental.pallas import tpu as pltpu
from jax.sharding import PartitionSpec as P

MESH = pl.DeviceIdType.MESH
F32 = jnp.float32
BF16 = jnp.bfloat16
VARS, NZ, ROWS, COLS = 3, 16, 64, 128
PLANES = VARS * NZ
CLASS = 12
MESSAGES = 80

SMOOTH = {0: 0.75, -2: -0.125, 2: -0.125, -1: 0.25, 1: 0.25}
DETAIL = {0: -0.5, 1: 1.0, 2: -0.5}


def lane_filters():
    def cell(x):
        return x if x >= 0 else 144 + x

    first = np.zeros((256, 256), np.float32)
    for k in range(-2, 67):
        for t, w in SMOOTH.items():
            first[cell(2 * k + t), k + 2] += w
        for t, w in DETAIL.items():
            first[cell(2 * k + t), 128 + k + 2] += w
    second = np.zeros((128, 128), np.float32)
    for m in range(0, 33):
        for t, w in SMOOTH.items():
            second[2 * m + t + 2, m + 2] += w
    for m in range(-1, 33):
        for t, w in DETAIL.items():
            second[2 * m + t + 2, 64 + m + 2] += w

    def inverse(count, out, offset, smooth, detail):
        matrix = np.zeros((2 * smooth(-2) + 2 * detail(-2), out), np.float32)
        for x in range(count):
            k, odd = divmod(x, 2)
            col = x + offset
            if odd:
                matrix[smooth(k), col] += 0.5
                matrix[smooth(k + 1), col] += 0.5
                matrix[detail(k), col] += 0.75
                matrix[detail(k - 1), col] -= 0.125
                matrix[detail(k + 1), col] -= 0.125
            else:
                matrix[smooth(k), col] += 1.0
                matrix[detail(k - 1), col] -= 0.25
                matrix[detail(k), col] -= 0.25
        return matrix

    back_first = inverse(128, 128, 0, lambda k: k + 2, lambda k: 128 + k + 2)
    back_second = inverse(65, 128, 2, lambda k: k + 2, lambda k: 64 + k + 2)
    packed = np.zeros((512, 256), np.float32)
    packed[:256] = first
    packed[256:, :128] = back_first
    packed[256:384, 128:] = second
    packed[384:, 128:] = back_second
    return packed.astype(BF16)


def halves(x):
    high = x.astype(BF16)
    low = (x - high.astype(F32)).astype(BF16)
    return high, low


def split_dot(x, filters):
    high, low = halves(x)
    return jnp.dot(high, filters, preferred_element_type=F32) + jnp.dot(low, filters, preferred_element_type=F32)


def forward_planes(x):
    count = len(x) // 2
    detail = []
    for k in range(count):
        after = x[2 * k + 2] if k + 1 < count else x[2 * count - 2]
        detail.append(x[2 * k + 1] - 0.5 * (x[2 * k] + after))
    smooth = [x[2 * k] + 0.25 * (detail[max(k - 1, 0)] + detail[k]) for k in range(count)]
    return smooth, detail


def inverse_planes(smooth, detail):
    count = len(smooth)
    even = [smooth[k] - 0.25 * (detail[max(k - 1, 0)] + detail[k]) for k in range(count)]
    out = []
    for k in range(count):
        out += [even[k], detail[k] + 0.5 * (even[k] + even[min(k + 1, count - 1)])]
    return out


def plane_slots(var):
    smooth = [4 * var + k for k in range(4)]
    middle = [12 + 4 * var + k for k in range(4)]
    fine = [24 + 8 * var + k for k in range(8)]
    return smooth, middle, fine


def kernel(
    field_ref, mk_ref, filt_ref, restored_ref, g_ref,
    x_ref, w_ref, t_ref, rp_ref, lp_ref, hl_ref, hr_ref, nk_ref, lhs_ref, y_ref, c_ref, s1_ref, s1l_ref, c2_ref,
    u_ref, m1_ref, m2_ref, own_ref, parts_ref, lhsi_ref, zr_ref, load_sem, send_sem, recv_sem,
):
    gx = lax.axis_index("gx")
    gy = lax.axis_index("gy")
    yy, xx = gx // 4, gx % 4
    zz, core = gy // 2, gy % 2
    group, low = gy // 4, zz % 2
    side = 2 * low - 1

    up, down = (gx + 15) % 16, (gx + 1) % 16
    left, right = (gy + 15) % 16, (gy + 1) % 16
    around = [(up, gy), (down, gy), (gx, left), (gx, right), (up, left), (up, right), (down, left), (down, right)]
    flip1 = gy + 1 - 2 * core
    flip2 = gy + 2 - 4 * low
    flip3 = flip2 + 1 - 2 * core
    sibling = (gx, flip1)
    pair = (gx, flip2)
    cross = (gx, (gy + 2 * side + 16) % 16)

    def along_x(k):
        return (yy * 4 + (xx + k) % 4, gy)

    def along_y(k):
        return (((yy + k) % 4) * 4 + xx, gy)

    def along_z(k):
        return (gx, (gy + 2 * side * k + 16) % 16)

    greeted = around + [(gx, flip1), (gx, flip2), (gx, flip3)]
    greeted += [along_x(k) for k in (1, 2, 3)] + [along_y(k) for k in (1, 2, 3)]
    greeted += [along_z(k) for k in (1, 2, -2, 3)]

    loads = [
        pltpu.make_async_copy(field_ref, x_ref, load_sem.at[0]),
        pltpu.make_async_copy(filt_ref, w_ref, load_sem.at[1]),
    ]
    for copy in loads:
        copy.start()
    barrier = pltpu.get_barrier_semaphore()
    for device in greeted:
        pl.semaphore_signal(barrier, inc=1, device_id=device, device_id_type=MESH)

    sent = []

    def send(src, dst, device):
        i = len(sent)
        copy = pltpu.make_async_remote_copy(
            src_ref=src, dst_ref=dst, send_sem=send_sem.at[i], recv_sem=recv_sem.at[i],
            device_id=device, device_id_type=MESH,
        )
        copy.start()
        sent.append(copy)
        return copy

    lane = lax.broadcasted_iota(jnp.int32, (1, 128), 1)

    loads[0].wait()
    for var in range(VARS):
        slots = plane_slots(var)

        def lift(tile, _, var=var, slots=slots):
            rows = pl.ds(pl.multiple_of(tile * 8, 8), 8)
            x = [x_ref[var * NZ + k, rows, :] for k in range(NZ)]
            smooth, fine = forward_planes(x)
            smooth, middle = forward_planes(smooth)
            ext = pl.ds(pl.multiple_of(tile * 8 + 8, 8), 8)
            for slot, value in zip(slots[0] + slots[1] + slots[2], smooth + middle + fine):
                t_ref[slot, ext, :] = value
            return _

        lax.fori_loop(0, 8, lift, None)

    def pack(q):
        rightward = jnp.zeros((ROWS, 128), F32)
        leftward = jnp.zeros((ROWS, 128), F32)
        for j in range(CLASS):
            plane = t_ref[q * CLASS + j, 8:72, :]
            here = (lane >= 8 * j) & (lane < 8 * j + 8)
            rightward = jnp.where(here, pltpu.roll(plane, (8 * j + 8) % 128, 1), rightward)
            leftward = jnp.where(here, pltpu.roll(plane, 8 * j, 1) if j else plane, leftward)
        rp_ref[q] = rightward
        lp_ref[q] = leftward

    def send_halo(q, n):
        p = pl.ds(q * CLASS, n * CLASS)
        c = pl.ds(q, n)
        return [
            send(rp_ref.at[c], hl_ref.at[c, 8:72], (gx, right)),
            send(lp_ref.at[c], hr_ref.at[c, 8:72], (gx, left)),
            send(t_ref.at[p, 64:72], t_ref.at[p, 0:8], (down, gy)),
            send(t_ref.at[p, 8:16], t_ref.at[p, 72:80], (up, gy)),
            send(rp_ref.at[c, 56:64], hl_ref.at[c, 0:8], (down, right)),
            send(rp_ref.at[c, 0:8], hl_ref.at[c, 72:80], (up, right)),
            send(lp_ref.at[c, 56:64], hr_ref.at[c, 0:8], (down, left)),
            send(lp_ref.at[c, 0:8], hr_ref.at[c, 72:80], (up, left)),
        ]

    pack(0)
    pl.semaphore_wait(barrier, len(greeted))
    halo0 = send_halo(0, 1)
    masks_in = [send(mk_ref, nk_ref.at[n], device) for n, device in enumerate(around)]
    for q in (1, 2, 3):
        pack(q)
    halo1 = send_halo(1, 3)
    loads[1].wait()

    def expand_masks():
        for copy in masks_in:
            copy.wait_recv()
        below, above, from_right, from_left, below_right, below_left, above_right, above_left = (
            nk_ref.at[n] for n in range(8)
        )
        bands = [(above_left, above, above_right, 1), (from_left, mk_ref, from_right, 0),
                 (from_left, mk_ref, from_right, 1), (below_left, below, below_right, 0)]
        wide = [[], []]
        for a, b, c, i in bands:
            wide[0].append(jnp.where(
                lane < 2, pltpu.roll(a[0, i], 66, 1),
                jnp.where(lane < 66, pltpu.roll(b[0, i], 2, 1), pltpu.roll(c[0, i], 66, 1))))
            base = jnp.where(
                lane < 2, pltpu.roll(a[1, i], 98, 1),
                jnp.where(lane < 34, pltpu.roll(b[1, i], 2, 1), pltpu.roll(c[1, i], 34, 1)))
            wide[1].append((base, pltpu.roll(base, 64, 1)))
        row = lax.broadcasted_iota(jnp.int32, (40, 128), 0)

        def by_rows(values, edges, count):
            out = jnp.broadcast_to(values[0], (count, 128))
            for value, edge in zip(values[1:], edges):
                out = jnp.where(row[:count] >= edge, jnp.broadcast_to(value, (count, 128)), out)
            return out

        for bz in range(2):
            for rd in range(2):
                for ld in range(2):
                    b = 4 * bz + 2 * ld + rd
                    m1_ref[bz, rd, :, 128 * ld:128 * ld + 128] = by_rows(
                        [v[b:b + 1] for v in wide[0]], (3, 19, 35), 40)
                b = 4 * bz + rd
                values = [jnp.where(lane < 64, v[b:b + 1], w[b + 2:b + 3]) for v, w in wide[1]]
                m2_ref[bz, rd] = by_rows(values, (rd, 8 + rd, 16 + rd), 24)

    def lanes1(q):
        for j in range(CLASS):
            sides = jnp.where(
                lane < 8, pltpu.roll(hr_ref[q], (128 - 8 * j) % 128, 1) if j else hr_ref[q],
                pltpu.roll(hl_ref[q], (136 - 8 * j) % 128, 1))
            for col, value in ((0, t_ref[q * CLASS + j]), (128, sides)):
                high, low_part = halves(value)
                lhs_ref[80 * j:80 * j + 80, col:col + 128] = high
                lhs_ref[80 * j:80 * j + 80, 256 + col:384 + col] = low_part
        filters = w_ref[0:256, :]
        both = jnp.concatenate([filters, filters], 0)

        def step(i, _):
            rows = pl.ds(pl.multiple_of(i * 320, 320), 320)
            out = jnp.dot(lhs_ref[rows, :], both, preferred_element_type=F32)
            for half in range(2):
                y_ref[pl.ds(q * CLASS + 4 * i, 4), half, 0:80, :] = out[:, 128 * half:128 * half + 128].reshape(4, 80, 128)
            return _

        lax.fori_loop(0, 3, step, None)

    def rows1(q):
        bz = 0 if q < 2 else 1

        def one(p):
            for half in range(2):
                cols = slice(128 * half, 128 * half + 128)
                even0, even1, even2 = (y_ref[p, half, pl.ds(s, 40, stride=2), :] for s in (0, 2, 4))
                odd0, odd1 = (y_ref[p, half, pl.ds(s, 40, stride=2), :] for s in (1, 3))
                detail = odd1 - 0.5 * (even1 + even2)
                before = odd0 - 0.5 * (even0 + even1)
                smooth = even1 + 0.25 * (before + detail)
                c_ref[p, 1, 0:40, cols] = detail * m1_ref[bz, 1, :, cols]
                if q < 2 and half == 0:
                    s1_ref[p] = smooth
                else:
                    c_ref[p, 0, 0:40, cols] = smooth * m1_ref[bz, 0, :, cols]

        def step(i, _):
            one(q * CLASS + 2 * i)
            one(q * CLASS + 2 * i + 1)
            return _

        lax.fori_loop(0, CLASS // 2, step, None)

    def lanes2(q):
        x = s1_ref[q * CLASS:(q + 1) * CLASS].reshape(CLASS * 40, 128)
        s1l_ref[q * CLASS:(q + 1) * CLASS, 0:40, :] = split_dot(x, w_ref[256:384, 128:256]).reshape(CLASS, 40, 128)

    def rows2(q):
        for p in range(q * CLASS, (q + 1) * CLASS):
            even0, even1, even2 = (s1l_ref[p, pl.ds(s, 24, stride=2), :] for s in (1, 3, 5))
            odd0, odd1 = (s1l_ref[p, pl.ds(s, 24, stride=2), :] for s in (2, 4))
            before = odd0 - 0.5 * (even0 + even1)
            detail = odd1 - 0.5 * (even1 + even2)
            smooth = even1 + 0.25 * (before + detail)
            if q == 0:
                local = jnp.where((lane >= 2) & (lane < 34), smooth[0:16], 0.0)
                own_ref[p] = pltpu.roll(local, (32 * (gy % 4) + 126) % 128, 1)
            c2_ref[p, 0, 0:24] = smooth * m2_ref[q, 0]
            c2_ref[p, 1, 0:24] = before * m2_ref[q, 1]

    def back2(q):
        for p in range(q * CLASS, (q + 1) * CLASS):
            smooth0, smooth1 = (c2_ref[p, 0, s:s + 24, :] for s in (0, 1))
            detail0, detail1, detail2 = (c2_ref[p, 1, s:s + 24, :] for s in (0, 1, 2))
            even = smooth0 - 0.25 * (detail0 + detail1)
            after = smooth1 - 0.25 * (detail1 + detail2)
            u_ref[p, pl.ds(3, 24, stride=2), :] = even
            u_ref[p, pl.ds(4, 24, stride=2), :] = detail1 + 0.5 * (even + after)
        x = u_ref[q * CLASS:(q + 1) * CLASS, 0:40, :].reshape(CLASS * 40, 128)
        c_ref[q * CLASS:(q + 1) * CLASS, 0, 0:40, 0:128] = split_dot(x, w_ref[384:512, 128:256]).reshape(CLASS, 40, 128)

    def back1(q):
        def one(p, j):
            for half in range(2):
                cols = slice(128 * half, 128 * half + 128)
                smooth0, smooth1 = (c_ref[p, 0, s:s + 32, cols] for s in (3, 4))
                detail0, detail1, detail2 = (c_ref[p, 1, s:s + 32, cols] for s in (2, 3, 4))
                even = smooth0 - 0.25 * (detail0 + detail1)
                after = smooth1 - 0.25 * (detail1 + detail2)
                odd = detail1 + 0.5 * (even + after)
                for which, value in ((0, even), (1, odd)):
                    rows = pl.ds(pl.multiple_of(j * 64 + 32 * which, 32), 32)
                    high, low_part = halves(value)
                    lhsi_ref[rows, cols] = high
                    lhsi_ref[rows, slice(256 + 128 * half, 384 + 128 * half)] = low_part

        def step(i, _):
            one(q * CLASS + 2 * i, 2 * i)
            one(q * CLASS + 2 * i + 1, 2 * i + 1)
            return _

        lax.fori_loop(0, CLASS // 2, step, None)
        filters = w_ref[256:512, 0:128]
        both = jnp.concatenate([filters, filters], 0)

        def multiply(i, _):
            rows = pl.ds(pl.multiple_of(i * 256, 256), 256)
            out = jnp.dot(lhsi_ref[rows, :], both, preferred_element_type=F32)
            zr_ref[pl.ds(q * CLASS + 4 * i, 4)] = out.reshape(4, 64, 128)
            return _

        lax.fori_loop(0, 3, multiply, None)

    def finish():
        for var in range(VARS):
            slots = plane_slots(var)
            for odd in range(2):
                for tile in range(4):
                    rows = slice(32 * odd + 8 * tile, 32 * odd + 8 * tile + 8)
                    smooth, middle, fine = ([zr_ref[p, rows, :] for p in part] for part in slots)
                    out = inverse_planes(inverse_planes(smooth, middle), fine)
                    for k in range(NZ):
                        restored_ref[var * NZ + k, pl.ds(16 * tile + odd, 8, stride=2), :] = out[k]

    def lanes_of(block):
        return pl.ds(pl.multiple_of(128 * ((block + 4) % 4), 128), 128)

    base = 6 * core
    p0, p1, p2 = (pl.ds(base + 2 * r, 2) for r in range(3))

    def both_ways(view, step):
        src = view(0)
        return send(src, src, step(1)), send(src, src, step(3))

    def pass_on(view, half_view, step, came):
        came[0].wait_recv()
        a = half_view(0, -1)
        first = send(a, a, step(1))
        came[1].wait_recv()
        b = half_view(1, 1)
        return first, send(b, b, step(3))

    def to_sibling(ref):
        return send(ref, ref, sibling)

    expand_masks()
    for copy in halo0:
        copy.wait_recv()
    lanes1(0)
    rows1(0)
    lanes2(0)
    rows2(0)
    other = 1 - core
    pre = [
        send(own_ref.at[pl.ds(6 * other, 6)], parts_ref.at[0], (gx, flip1)),
        send(own_ref.at[pl.ds(6 * core, 6)], parts_ref.at[1], (gx, flip2)),
        send(own_ref.at[pl.ds(6 * other, 6)], parts_ref.at[2], (gx, flip3)),
    ]
    for copy in halo1:
        copy.wait_recv()
    for copy in pre:
        copy.wait_recv()
    block = own_ref[pl.ds(base, 6)] + parts_ref[0] + parts_ref[1] + parts_ref[2]
    g_ref[pl.ds(base, 6), yy, xx, :, lanes_of(group)] = block

    mine0 = g_ref.at[p0, yy, xx, :, lanes_of(group)]
    xs = [send(mine0, mine0, along_x(k)) for k in (1, 3, 2)]
    mine12 = g_ref.at[pl.ds(base + 2, 4), yy, xx, :, lanes_of(group)]
    zs = [send(mine12, mine12, along_z(k)) for k in (1, 2, 3)]

    lanes1(1)
    rows1(1)

    def y0(k):
        return g_ref.at[p0, (yy + k + 4) % 4, :, :, lanes_of(group)]

    def y0_half(h, k):
        return g_ref.at[base + h, (yy + k + 4) % 4, :, :, lanes_of(group)]

    def x1(k):
        return g_ref.at[p1, yy, (xx + k + 4) % 4]

    def x1_half(h, k):
        return g_ref.at[base + 2 + h, yy, (xx + k + 4) % 4]

    def y2(k):
        return g_ref.at[p2, (yy + k + 4) % 4, xx]

    def y2_half(h, k):
        return g_ref.at[base + 4 + h, (yy + k + 4) % 4, xx]

    for copy in xs:
        copy.wait_recv()
    a0 = both_ways(y0, along_y)
    for copy in zs:
        copy.wait_recv()
    a1 = both_ways(x1, along_x)
    a2 = both_ways(y2, along_y)
    lanes2(1)
    rows2(1)
    f0 = pass_on(y0, y0_half, along_y, a0)
    f1 = pass_on(x1, x1_half, along_x, a1)
    f2 = pass_on(y2, y2_half, along_y, a2)
    back2(0)

    def z0(k):
        return g_ref.at[p0, :, :, :, lanes_of(group + k)]

    def z0_half(h, k):
        return g_ref.at[base + h, :, :, :, lanes_of(group + k)]

    def y1(k):
        return g_ref.at[p1, (yy + k + 4) % 4]

    def y1_half(h, k):
        return g_ref.at[base + 2 + h, (yy + k + 4) % 4]

    def x2(k):
        return g_ref.at[p2, :, (xx + k + 4) % 4]

    def x2_half(h, k):
        return g_ref.at[base + 4 + h, :, (xx + k + 4) % 4]

    for copy in f0:
        copy.wait_recv()
    c1 = send(z0(0), z0(0), cross)
    for copy in f1:
        copy.wait_recv()
    b1 = both_ways(y1, along_y)
    for copy in f2:
        copy.wait_recv()
    b2 = both_ways(x2, along_x)
    sib = [to_sibling(z0(0)), to_sibling(y1(0)), to_sibling(x2(0))]
    back2(1)
    lanes1(2)
    rows1(2)
    c1.wait_recv()
    c2 = send(z0(side), z0(side), pair)
    sib.append(to_sibling(z0(side)))
    e1 = pass_on(y1, y1_half, along_y, b1)
    e2 = pass_on(x2, x2_half, along_x, b2)
    for view in (y1, x2):
        sib += [to_sibling(view(-1)), to_sibling(view(1))]
    lanes1(3)
    rows1(3)
    c2.wait_recv()
    c3 = send(z0_half(1 - low, -side), z0_half(1 - low, -side), cross)
    sib.append(to_sibling(z0(-side)))
    back1(0)
    back1(1)
    c3.wait_recv()
    c4 = send(z0_half(low, 2), z0_half(low, 2), pair)
    for copy in e1:
        copy.wait_recv()
    sib.append(to_sibling(y1(2)))
    for copy in e2:
        copy.wait_recv()
    sib.append(to_sibling(x2(2)))
    back1(2)
    back1(3)
    c4.wait_recv()
    sib.append(to_sibling(z0(2)))
    finish()
    for copy in sib:
        copy.wait_recv()
    for copy in sent:
        copy.wait_send()


def body(field, masks):
    flags = masks.astype(F32)
    level1 = jnp.pad(jnp.repeat(flags[0], 16, 2), ((1, 0), (0, 0), (0, 64)), constant_values=1.0)
    level2 = jnp.pad(jnp.repeat(flags[1], 8, 2), ((1, 0), (0, 0), (0, 96)), constant_values=1.0)
    mk = jnp.stack([level1, level2]).transpose(0, 2, 1, 3)
    anywhere = pl.BlockSpec(memory_space=pl.ANY)
    in_vmem = pl.BlockSpec(memory_space=pltpu.VMEM)
    restored, coarse = pl.pallas_call(
        kernel,
        out_shape=(
            jax.ShapeDtypeStruct((PLANES, ROWS, COLS), F32),
            jax.ShapeDtypeStruct((12, 4, 4, 16, 512), F32),
        ),
        in_specs=[anywhere, in_vmem, anywhere],
        out_specs=(in_vmem, in_vmem),
        scratch_shapes=[
            pltpu.VMEM((PLANES, ROWS, COLS), F32),
            pltpu.VMEM((512, 256), BF16),
            pltpu.VMEM((PLANES, 80, 128), F32),
            pltpu.VMEM((4, ROWS, 128), F32),
            pltpu.VMEM((4, ROWS, 128), F32),
            pltpu.VMEM((4, 80, 128), F32),
            pltpu.VMEM((4, 80, 128), F32),
            pltpu.VMEM((8, 2, 2, 8, 128), F32),
            pltpu.VMEM((CLASS * 80, 512), BF16),
            pltpu.VMEM((PLANES, 2, 88, 128), F32),
            pltpu.VMEM((PLANES, 2, 40, 256), F32),
            pltpu.VMEM((2 * CLASS, 40, 128), F32),
            pltpu.VMEM((2 * CLASS, 56, 128), F32),
            pltpu.VMEM((2 * CLASS, 2, 32, 128), F32),
            pltpu.VMEM((2 * CLASS, 56, 128), F32),
            pltpu.VMEM((2, 2, 40, 256), F32),
            pltpu.VMEM((2, 2, 24, 128), F32),
            pltpu.VMEM((CLASS, 16, 128), F32),
            pltpu.VMEM((3, 6, 16, 128), F32),
            pltpu.VMEM((CLASS * 64, 512), BF16),
            pltpu.VMEM((PLANES, 64, 128), F32),
            pltpu.SemaphoreType.DMA((2,)),
            pltpu.SemaphoreType.DMA((MESSAGES,)),
            pltpu.SemaphoreType.DMA((MESSAGES,)),
        ],
        compiler_params=pltpu.CompilerParams(
            collective_id=0, has_side_effects=True, vmem_limit_bytes=48 * 1024 * 1024
        ),
        cost_estimate=pl.CostEstimate(flops=2_000_000_000, bytes_accessed=10_000_000, transcendentals=0),
    )(field.reshape(PLANES, ROWS, COLS), mk, jnp.asarray(lane_filters()))
    return restored.reshape(VARS, NZ, ROWS, COLS), coarse.reshape(VARS, 4, 256, 512)


def solution(mesh):
    placed = (P(None, None, "gx", "gy"), P(None, None, "gx", "gy"))
    return jax.shard_map(
        body,
        mesh=mesh,
        in_specs=placed,
        out_specs=(P(None, None, "gx", "gy"), P()),
        check_vma=False,
    )
```

time: 351 us -> 71.2 us (0.20); the launches traced: 345 us -> 71 us
  local copies, waits for them, and re-layouts: 210 us -> 10.2 us
  Pallas kernels: 0 us -> 59.3 us
  other arithmetic: 46.4 us -> 0.7 us
  starting transfers between devices: 33 us -> 0 us
  blocking collectives: 23.7 us -> 0 us
  waiting for transfers between devices: 17.3 us -> 0 us
  between operations: 15 us -> 0.7 us
    slice x35 -> x0, local copies, waits for them, and re-layouts: 168 us -> none  [the longest x16 137 us: take_slice(): return lax.slice_in_dim(volume, start, stop, stride, direction)]
    pallas_call x0 -> x1, Pallas kernels: none -> 59.3 us  [body(): pl.pallas_call(kernel, out_shape=(jax.ShapeDtypeStruct((PLANES, ROWS, COL...]
    ppermute x16 -> x0, starting transfers between devices: 32.9 us -> none  [the longest x8 22.6 us: extended(): after = lax.ppermute(leading, axis, down)]
    all_to_all x1 -> x0, blocking collectives: 23.7 us -> none  [from_everyone(): lax.all_to_all(jnp.broadcast_to(x[None], (count, *x.shape)), axis, 0, 0,...]
    ppermute x16 -> x0, waiting for transfers between devices: 17.2 us -> none  [the longest x8 13.1 us: extended(): before = lax.ppermute(last, axis, up)]
    sub x18 -> x0, other arithmetic: 16.5 us -> none  [the longest x6 7.13 us: lift_inverse(): take_slice(smooth_pad, 1, length + 2, 1, direction)]
    ppermute x6 -> x0, local copies, waits for them, and re-layouts: 15.2 us -> none  [the longest x3 8.02 us: extended(): before = lax.ppermute(last, axis, up)]
    concatenate x14 -> x0, other arithmetic: 13.7 us -> none  [the longest x8 12.4 us: extended(): x = jnp.concatenate([before, x, after], axis=dim)]
  transfers between devices with their start and end apart: 17 -> 0, of which waited for: 9 -> 0; matrix products, arithmetic and copies ran while one was open for 23% -> 0% of each run, Pallas kernels for 0% -> 0%
where the time goes in v1:
time: 71.2 us; the launch traced here: 71 us
  Pallas kernels  59.3 us (83%)
  local copies, waits for them, and re-layouts  10.2 us (14%)
    pallas_call x1, Pallas kernels, body(): pl.pallas_call(kernel, out_shape=(jax.ShapeDtypeStruct((PLANES, ROWS, COL...  59.3 us
    unnamed x6, local copies, waits for them, and re-layouts  9.69 us

profile of v1, /device:TPU:1, one launch (start us, length us, event | category | flops | bytes accessed | tf_op | source)
XLA Modules:
  0.0 71.0 jit_solution(10926758783416495679)
XLA Ops:
  0.6 0.7 convert_element_type.3
  1.3 0.1 copy.7
  1.4 0.1 copy.9
  1.5 0.1 broadcast_in_dim.7
  1.6 0.1 reshape.21
  1.7 0.1 broadcast_in_dim.6
  1.8 0.1 reshape.20
  1.9 0.0 copy-start
  1.9 1.4 %copy-done = f32[3,16,64,128]{3,2,1,0:T(8,128)S(1)} copy-done((f32[3,16,64,128]{3,2,1,0:T(8,128)S(1)}, f32[3,16,64,128]{3,2,1,0:T(8,128)}, u32[]{:S(2)}) %copy-start) | copy-done | bytes 1572888
  3.3 0.0 copy-start.1
  3.4 0.9 %copy-done.1 = bf16[512,256]{1,0:T(8,128)(2,1)S(1)} copy-done((bf16[512,256]{1,0:T(8,128)(2,1)S(1)}, bf16[512,256]{1,0:T(8,128)(2,1)}, u32[]{:S(2)}) %copy-start.1) | copy-done | bytes 262168
  4.3 59.3 %shard_map.50 = (f32[48,64,128]{2,1,0:T(8,128)S(1)}, f32[12,4,4,16,512]{4,3,2,1,0:T(8,128)}) custom-call(f32[48,64,128]{2,1,0:T(8,128)S(1)} %bitcast.14, f32[2,2,8,128]{3,2,1,0:T(8,128)S(1)} %maximum_bitcast_fusion.mk_ref, bf16[512,256]{1,0:T(8,128)(2,1)S(1)} %copy-done.1), custom_call_target="tpu_custom_call" | custom-call | flops 2000000000 | bytes 10000000 | tf_op jit(solution)/shard_map/pallas_call | solution.py:515
  63.6 1.1 %copy.13 = f32[3,16,64,128]{3,2,1,0:T(8,128)} copy(f32[3,16,64,128]{3,2,1,0:T(8,128)S(1)} %bitcast.13) | data formatting | bytes 3145728
  64.8 6.2 %copy.14 = f32[3,4,256,512]{3,2,1,0:T(8,128)} copy(f32[3,4,256,512]{3,2,1,0:T(8,128)} %bitcast.15) | data formatting | bytes 12582912
  (5 shorter events, 0.0 us)
Async XLA Ops:
  1.9 1.4 %copy-start = (f32[3,16,64,128]{3,2,1,0:T(8,128)S(1)}, f32[3,16,64,128]{3,2,1,0:T(8,128)}, u32[]{:S(2)}) copy-start(f32[3,16,64,128]{3,2,1,0:T(8,128)} %param.3) | copy-start | bytes 4718596
  3.3 0.9 %copy-start.1 = (bf16[512,256]{1,0:T(8,128)(2,1)S(1)}, bf16[512,256]{1,0:T(8,128)(2,1)}, u32[]{:S(2)}) copy-start(bf16[512,256]{1,0:T(8,128)(2,1)} %constant.4.clone.filt_ref) | copy-start | bytes 786436

commit v2 on v1

--- a/solution.py
+++ b/solution.py
@@ -1,6 +1,5 @@
 import jax
 import jax.numpy as jnp
-import numpy as np
 from jax import lax
 from jax.experimental import pallas as pl
 from jax.experimental.pallas import tpu as pltpu
@@ -12,55 +11,38 @@
 VARS, NZ, ROWS, COLS = 3, 16, 64, 128
 PLANES = VARS * NZ
 CLASS = 12
-MESSAGES = 80
-
-SMOOTH = {0: 0.75, -2: -0.125, 2: -0.125, -1: 0.25, 1: 0.25}
-DETAIL = {0: -0.5, 1: 1.0, 2: -0.5}
-
-
-def lane_filters():
-    def cell(x):
-        return x if x >= 0 else 144 + x
-
-    first = np.zeros((256, 256), np.float32)
-    for k in range(-2, 67):
-        for t, w in SMOOTH.items():
-            first[cell(2 * k + t), k + 2] += w
-        for t, w in DETAIL.items():
-            first[cell(2 * k + t), 128 + k + 2] += w
-    second = np.zeros((128, 128), np.float32)
-    for m in range(0, 33):
-        for t, w in SMOOTH.items():
-            second[2 * m + t + 2, m + 2] += w
-    for m in range(-1, 33):
-        for t, w in DETAIL.items():
-            second[2 * m + t + 2, 64 + m + 2] += w
-
-    def inverse(count, out, offset, smooth, detail):
-        matrix = np.zeros((2 * smooth(-2) + 2 * detail(-2), out), np.float32)
-        for x in range(count):
-            k, odd = divmod(x, 2)
-            col = x + offset
-            if odd:
-                matrix[smooth(k), col] += 0.5
-                matrix[smooth(k + 1), col] += 0.5
-                matrix[detail(k), col] += 0.75
-                matrix[detail(k - 1), col] -= 0.125
-                matrix[detail(k + 1), col] -= 0.125
-            else:
-                matrix[smooth(k), col] += 1.0
-                matrix[detail(k - 1), col] -= 0.25
-                matrix[detail(k), col] -= 0.25
-        return matrix
-
-    back_first = inverse(128, 128, 0, lambda k: k + 2, lambda k: 128 + k + 2)
-    back_second = inverse(65, 128, 2, lambda k: k + 2, lambda k: 64 + k + 2)
-    packed = np.zeros((512, 256), np.float32)
-    packed[:256] = first
-    packed[256:, :128] = back_first
-    packed[256:384, 128:] = second
-    packed[384:, 128:] = back_second
-    return packed.astype(BF16)
+MESSAGES = 128
+VMEM_LIMIT = 32 * 1024 * 1024
+
+
+def by_distance(distance, taps):
+    out = jnp.zeros(distance.shape, F32)
+    for at, weight in taps.items():
+        out = jnp.where(distance == at, weight, out)
+    return out
+
+
+FORWARD_SMOOTH = {0: 0.75, -2: -0.125, 2: -0.125, -1: 0.25, 1: 0.25}
+FORWARD_DETAIL = {0: -0.5, 1: 1.0, 2: -0.5}
+INVERSE_SMOOTH = {0: 1.0, -1: 0.5, 1: 0.5}
+INVERSE_DETAIL = {1: 0.75, 0: -0.25, 2: -0.25, -1: -0.125, 3: -0.125}
+
+
+def write_filters(w_ref):
+    row = lax.broadcasted_iota(jnp.int32, (256, 128), 0)
+    col = lax.broadcasted_iota(jnp.int32, (256, 128), 1)
+    cell = jnp.where(row < 136, row, jnp.where(row < 144, row - 144, 4096))
+    w_ref[0:256, 0:128] = by_distance(cell - 2 * (col - 2), FORWARD_SMOOTH).astype(BF16)
+    w_ref[0:256, 128:256] = by_distance(cell - 2 * (col - 2), FORWARD_DETAIL).astype(BF16)
+    w_ref[256:384, 0:128] = by_distance(col[:128] - 2 * (row[:128] - 2), INVERSE_SMOOTH).astype(BF16)
+    w_ref[384:512, 0:128] = by_distance(col[:128] - 2 * (row[:128] - 2), INVERSE_DETAIL).astype(BF16)
+    row, col = row[:128], col[:128]
+    ahead = row - 2 - 2 * (jnp.where(col < 64, col, col - 64) - 2)
+    w_ref[256:384, 128:256] = jnp.where(
+        col < 64, by_distance(ahead, FORWARD_SMOOTH), by_distance(ahead, FORWARD_DETAIL)).astype(BF16)
+    ahead = col - 2 - 2 * (jnp.where(row < 64, row, row - 64) - 2)
+    w_ref[384:512, 128:256] = jnp.where(
+        row < 64, by_distance(ahead, INVERSE_SMOOTH), by_distance(ahead, INVERSE_DETAIL)).astype(BF16)
 
 
 def halves(x):
@@ -101,9 +83,9 @@
 
 
 def kernel(
-    field_ref, mk_ref, filt_ref, restored_ref, g_ref,
-    x_ref, w_ref, t_ref, rp_ref, lp_ref, hl_ref, hr_ref, nk_ref, lhs_ref, y_ref, c_ref, s1_ref, s1l_ref, c2_ref,
-    u_ref, m1_ref, m2_ref, own_ref, parts_ref, lhsi_ref, zr_ref, load_sem, send_sem, recv_sem,
+    field_ref, masks_ref, restored_ref, g_ref,
+    x_ref, mk_ref, w_ref, t_ref, rp_ref, lp_ref, hl_ref, hr_ref, nk_ref, lhs_ref, y_ref, c_ref, s1_ref, s1l_ref, c2_ref,
+    u_ref, m1_ref, m2_ref, own_ref, parts_ref, lhsi_ref, zr_ref, j_ref, load_sem, send_sem, recv_sem,
 ):
     gx = lax.axis_index("gx")
     gy = lax.axis_index("gy")
@@ -136,15 +118,17 @@
     greeted += [along_z(k) for k in (1, 2, -2, 3)]
 
     loads = [
-        pltpu.make_async_copy(field_ref, x_ref, load_sem.at[0]),
-        pltpu.make_async_copy(filt_ref, w_ref, load_sem.at[1]),
+        pltpu.make_async_copy(field_ref.at[NZ * v:NZ * v + NZ], x_ref.at[NZ * v:NZ * v + NZ], load_sem.at[v])
+        for v in range(VARS)
     ]
+    loads.append(pltpu.make_async_copy(masks_ref, mk_ref, load_sem.at[VARS]))
     for copy in loads:
         copy.start()
     barrier = pltpu.get_barrier_semaphore()
     for device in greeted:
         pl.semaphore_signal(barrier, inc=1, device_id=device, device_id_type=MESH)
 
+    write_filters(w_ref)
     sent = []
 
     def send(src, dst, device):
@@ -159,9 +143,9 @@
 
     lane = lax.broadcasted_iota(jnp.int32, (1, 128), 1)
 
-    loads[0].wait()
     for var in range(VARS):
         slots = plane_slots(var)
+        loads[var].wait()
 
         def lift(tile, _, var=var, slots=slots):
             rows = pl.ds(pl.multiple_of(tile * 8, 8), 8)
@@ -203,11 +187,11 @@
     pack(0)
     pl.semaphore_wait(barrier, len(greeted))
     halo0 = send_halo(0, 1)
+    loads[VARS].wait()
     masks_in = [send(mk_ref, nk_ref.at[n], device) for n, device in enumerate(around)]
     for q in (1, 2, 3):
         pack(q)
     halo1 = send_halo(1, 3)
-    loads[1].wait()
 
     def expand_masks():
         for copy in masks_in:
@@ -217,15 +201,18 @@
         )
         bands = [(above_left, above, above_right, 1), (from_left, mk_ref, from_right, 0),
                  (from_left, mk_ref, from_right, 1), (below_left, below, below_right, 0)]
+        block = lax.broadcasted_iota(jnp.int32, (8, 128), 0)
+        place = lax.broadcasted_iota(jnp.int32, (8, 128), 1)
         wide = [[], []]
-        for a, b, c, i in bands:
-            wide[0].append(jnp.where(
-                lane < 2, pltpu.roll(a[0, i], 66, 1),
-                jnp.where(lane < 66, pltpu.roll(b[0, i], 2, 1), pltpu.roll(c[0, i], 66, 1))))
-            base = jnp.where(
-                lane < 2, pltpu.roll(a[1, i], 98, 1),
-                jnp.where(lane < 34, pltpu.roll(b[1, i], 2, 1), pltpu.roll(c[1, i], 34, 1)))
-            wide[1].append((base, pltpu.roll(base, 64, 1)))
+        for level, spread_out in enumerate(((place + 14) // 16 == block, (place % 64 + 6) // 8 == block)):
+            spread_out = jnp.where(spread_out, 1.0, 0.0)
+            for n, (a, b, c, i) in enumerate(bands):
+                j_ref[level, n] = jnp.zeros((8, 128), F32)
+                j_ref[level, n, 0:1, 0:7] = a[level, i, 3:4].astype(F32)
+                j_ref[level, n, 1:5, 0:7] = b[level, i].astype(F32)
+                j_ref[level, n, 5:6, 0:7] = c[level, i, 0:1].astype(F32)
+                wide[level].append(lax.dot_general(
+                    j_ref[level, n], spread_out, (((0,), (0,)), ((), ())), preferred_element_type=F32))
         row = lax.broadcasted_iota(jnp.int32, (40, 128), 0)
 
         def by_rows(values, edges, count):
@@ -237,14 +224,15 @@
         for bz in range(2):
             for rd in range(2):
                 for ld in range(2):
-                    b = 4 * bz + 2 * ld + rd
-                    m1_ref[bz, rd, :, 128 * ld:128 * ld + 128] = by_rows(
-                        [v[b:b + 1] for v in wide[0]], (3, 19, 35), 40)
-                b = 4 * bz + rd
-                values = [jnp.where(lane < 64, v[b:b + 1], w[b + 2:b + 3]) for v, w in wide[1]]
+                    b = 4 * bz + 2 * ld + rd - 1
+                    if b >= 0:
+                        m1_ref[bz, rd, :, 128 * ld:128 * ld + 128] = by_rows(
+                            [v[b:b + 1] for v in wide[0]], (3, 19, 35), 40)
+                b = 4 * bz + rd - 1
+                values = [jnp.where(lane < 64, v[b:b + 1] if b >= 0 else 1.0, v[b + 2:b + 3]) for v in wide[1]]
                 m2_ref[bz, rd] = by_rows(values, (rd, 8 + rd, 16 + rd), 24)
 
-    def lanes1(q):
+    def sides_and_halves(q):
         for j in range(CLASS):
             sides = jnp.where(
                 lane < 8, pltpu.roll(hr_ref[q], (128 - 8 * j) % 128, 1) if j else hr_ref[q],
@@ -253,17 +241,45 @@
                 high, low_part = halves(value)
                 lhs_ref[80 * j:80 * j + 80, col:col + 128] = high
                 lhs_ref[80 * j:80 * j + 80, 256 + col:384 + col] = low_part
-        filters = w_ref[0:256, :]
+
+    def lanes1(q, parts=(0, 1)):
+        cols = slice(128 * parts[0], 128 * parts[-1] + 128)
+        filters = w_ref[0:256, cols]
         both = jnp.concatenate([filters, filters], 0)
 
         def step(i, _):
             rows = pl.ds(pl.multiple_of(i * 320, 320), 320)
             out = jnp.dot(lhs_ref[rows, :], both, preferred_element_type=F32)
-            for half in range(2):
-                y_ref[pl.ds(q * CLASS + 4 * i, 4), half, 0:80, :] = out[:, 128 * half:128 * half + 128].reshape(4, 80, 128)
+            for n, half in enumerate(parts):
+                y_ref[pl.ds(q * CLASS + 4 * i, 4), half, 0:80, :] = out[:, 128 * n:128 * n + 128].reshape(4, 80, 128)
             return _
 
         lax.fori_loop(0, 3, step, None)
+
+    def smooth_rows1(q):
+        def one(p):
+            even0, even1, even2 = (y_ref[p, 0, pl.ds(s, 40, stride=2), :] for s in (0, 2, 4))
+            odd0, odd1 = (y_ref[p, 0, pl.ds(s, 40, stride=2), :] for s in (1, 3))
+            detail = odd1 - 0.5 * (even1 + even2)
+            before = odd0 - 0.5 * (even0 + even1)
+            s1_ref[p] = even1 + 0.25 * (before + detail)
+
+        def step(i, _):
+            for n in range(4):
+                one(q * CLASS + 4 * i + n)
+            return _
+
+        lax.fori_loop(0, CLASS // 4, step, None)
+
+    def coarse_rows2():
+        for p in range(CLASS):
+            even0, even1, even2 = (s1l_ref[p, pl.ds(s, 16, stride=2), :] for s in (1, 3, 5))
+            odd0, odd1 = (s1l_ref[p, pl.ds(s, 16, stride=2), :] for s in (2, 4))
+            detail = odd1 - 0.5 * (even1 + even2)
+            before = odd0 - 0.5 * (even0 + even1)
+            smooth = even1 + 0.25 * (before + detail)
+            local = jnp.where((lane >= 2) & (lane < 34), smooth, 0.0)
+            own_ref[p] = pltpu.roll(local, (32 * (gy % 4) + 126) % 128, 1)
 
     def rows1(q):
         bz = 0 if q < 2 else 1
@@ -277,9 +293,9 @@
                 before = odd0 - 0.5 * (even0 + even1)
                 smooth = even1 + 0.25 * (before + detail)
                 c_ref[p, 1, 0:40, cols] = detail * m1_ref[bz, 1, :, cols]
-                if q < 2 and half == 0:
+                if q == 1 and half == 0:
                     s1_ref[p] = smooth
-                else:
+                elif q > 1 or half == 1:
                     c_ref[p, 0, 0:40, cols] = smooth * m1_ref[bz, 0, :, cols]
 
         def step(i, _):
@@ -300,9 +316,6 @@
             before = odd0 - 0.5 * (even0 + even1)
             detail = odd1 - 0.5 * (even1 + even2)
             smooth = even1 + 0.25 * (before + detail)
-            if q == 0:
-                local = jnp.where((lane >= 2) & (lane < 34), smooth[0:16], 0.0)
-                own_ref[p] = pltpu.roll(local, (32 * (gy % 4) + 126) % 128, 1)
             c2_ref[p, 0, 0:24] = smooth * m2_ref[q, 0]
             c2_ref[p, 1, 0:24] = before * m2_ref[q, 1]
 
@@ -365,152 +378,147 @@
 
     base = 6 * core
     p0, p1, p2 = (pl.ds(base + 2 * r, 2) for r in range(3))
-
-    def both_ways(view, step):
-        src = view(0)
-        return send(src, src, step(1)), send(src, src, step(3))
-
-    def pass_on(view, half_view, step, came):
+    order = (1, 3, 2)
+
+    def strip0(ky, kz, plane=p0):
+        return g_ref.at[plane, (yy + ky + 4) % 4, :, :, lanes_of(group + kz)]
+
+    def strip1(kx, ky=0):
+        return g_ref.at[p1, (yy + ky + 4) % 4, (xx + kx + 4) % 4]
+
+    def strip2(ky, kx=0):
+        return g_ref.at[p2, (yy + ky + 4) % 4, (xx + kx + 4) % 4]
+
+    def spread(view, axis):
+        return [send(view, view, axis(k)) for k in order]
+
+    def ship0(ky):
+        whole = strip0(ky, 0)
+        half = strip0(ky, 0, base + low)
+        return send(whole, whole, cross), send(half, half, along_z(3))
+
+    def relay0(ky, came):
         came[0].wait_recv()
-        a = half_view(0, -1)
-        first = send(a, a, step(1))
+        whole = strip0(ky, side)
+        first = send(whole, whole, pair)
         came[1].wait_recv()
-        b = half_view(1, 1)
-        return first, send(b, b, step(3))
+        half = strip0(ky, 2, base + 1 - low)
+        return first, send(half, half, pair)
 
     def to_sibling(ref):
         return send(ref, ref, sibling)
 
-    expand_masks()
-    for copy in halo0:
-        copy.wait_recv()
-    lanes1(0)
-    rows1(0)
+    def arrived(copies):
+        for copy in copies:
+            copy.wait_recv()
+
+    arrived(halo0)
+    sides_and_halves(0)
+    lanes1(0, (0,))
+    smooth_rows1(0)
     lanes2(0)
-    rows2(0)
+    coarse_rows2()
     other = 1 - core
     pre = [
         send(own_ref.at[pl.ds(6 * other, 6)], parts_ref.at[0], (gx, flip1)),
         send(own_ref.at[pl.ds(6 * core, 6)], parts_ref.at[1], (gx, flip2)),
         send(own_ref.at[pl.ds(6 * other, 6)], parts_ref.at[2], (gx, flip3)),
     ]
-    for copy in halo1:
-        copy.wait_recv()
-    for copy in pre:
-        copy.wait_recv()
+    lanes1(0, (1,))
+    expand_masks()
+    arrived(pre)
     block = own_ref[pl.ds(base, 6)] + parts_ref[0] + parts_ref[1] + parts_ref[2]
     g_ref[pl.ds(base, 6), yy, xx, :, lanes_of(group)] = block
 
-    mine0 = g_ref.at[p0, yy, xx, :, lanes_of(group)]
-    xs = [send(mine0, mine0, along_x(k)) for k in (1, 3, 2)]
-    mine12 = g_ref.at[pl.ds(base + 2, 4), yy, xx, :, lanes_of(group)]
-    zs = [send(mine12, mine12, along_z(k)) for k in (1, 2, 3)]
-
+    xs = spread(g_ref.at[p0, yy, xx, :, lanes_of(group)], along_x)
+    zs = spread(g_ref.at[pl.ds(base + 2, 4), yy, xx, :, lanes_of(group)], along_z)
+    rows1(0)
+    arrived(halo1)
+    sides_and_halves(1)
     lanes1(1)
+
+    arrived(xs)
+    ys0 = spread(strip0(0, 0), along_y)
+    s0 = ship0(0)
     rows1(1)
-
-    def y0(k):
-        return g_ref.at[p0, (yy + k + 4) % 4, :, :, lanes_of(group)]
-
-    def y0_half(h, k):
-        return g_ref.at[base + h, (yy + k + 4) % 4, :, :, lanes_of(group)]
-
-    def x1(k):
-        return g_ref.at[p1, yy, (xx + k + 4) % 4]
-
-    def x1_half(h, k):
-        return g_ref.at[base + 2 + h, yy, (xx + k + 4) % 4]
-
-    def y2(k):
-        return g_ref.at[p2, (yy + k + 4) % 4, xx]
-
-    def y2_half(h, k):
-        return g_ref.at[base + 4 + h, (yy + k + 4) % 4, xx]
-
-    for copy in xs:
-        copy.wait_recv()
-    a0 = both_ways(y0, along_y)
-    for copy in zs:
-        copy.wait_recv()
-    a1 = both_ways(x1, along_x)
-    a2 = both_ways(y2, along_y)
     lanes2(1)
+
+    arrived(zs)
+    xs1 = spread(strip1(0), along_x)
+    ys2 = spread(strip2(0), along_y)
+    ys1 = {0: spread(strip1(0), along_y)}
+    xs2 = {0: spread(strip2(0), along_x)}
+    rows2(0)
     rows2(1)
-    f0 = pass_on(y0, y0_half, along_y, a0)
-    f1 = pass_on(x1, x1_half, along_x, a1)
-    f2 = pass_on(y2, y2_half, along_y, a2)
+
+    s0 = {0: s0}
+    for n, k in enumerate(order):
+        ys0[n].wait_recv()
+        s0[-k] = ship0(-k)
     back2(0)
-
-    def z0(k):
-        return g_ref.at[p0, :, :, :, lanes_of(group + k)]
-
-    def z0_half(h, k):
-        return g_ref.at[base + h, :, :, :, lanes_of(group + k)]
-
-    def y1(k):
-        return g_ref.at[p1, (yy + k + 4) % 4]
-
-    def y1_half(h, k):
-        return g_ref.at[base + 2 + h, (yy + k + 4) % 4]
-
-    def x2(k):
-        return g_ref.at[p2, :, (xx + k + 4) % 4]
-
-    def x2_half(h, k):
-        return g_ref.at[base + 4 + h, :, (xx + k + 4) % 4]
-
-    for copy in f0:
-        copy.wait_recv()
-    c1 = send(z0(0), z0(0), cross)
-    for copy in f1:
-        copy.wait_recv()
-    b1 = both_ways(y1, along_y)
-    for copy in f2:
-        copy.wait_recv()
-    b2 = both_ways(x2, along_x)
-    sib = [to_sibling(z0(0)), to_sibling(y1(0)), to_sibling(x2(0))]
+    r0 = {0: relay0(0, s0[0])}
+    for n, k in enumerate(order):
+        xs1[n].wait_recv()
+        ys1[-k] = spread(strip1(-k), along_y)
+        ys2[n].wait_recv()
+        xs2[-k] = spread(strip2(-k), along_x)
     back2(1)
+    sides_and_halves(2)
     lanes1(2)
     rows1(2)
-    c1.wait_recv()
-    c2 = send(z0(side), z0(side), pair)
-    sib.append(to_sibling(z0(side)))
-    e1 = pass_on(y1, y1_half, along_y, b1)
-    e2 = pass_on(x2, x2_half, along_x, b2)
-    for view in (y1, x2):
-        sib += [to_sibling(view(-1)), to_sibling(view(1))]
+    for k in order:
+        r0[-k] = relay0(-k, s0[-k])
+    sib = []
+
+    def complete(which):
+        arrived(ys1[which])
+        sib.append(to_sibling(g_ref.at[p1, :, (xx + which + 4) % 4]))
+        arrived(xs2[which])
+        sib.append(to_sibling(g_ref.at[p2, (yy + which + 4) % 4]))
+
+    def complete0(which):
+        arrived(r0[which])
+        sib.append(to_sibling(g_ref.at[p0, (yy + which + 4) % 4]))
+
+    complete(0)
+    sides_and_halves(3)
     lanes1(3)
     rows1(3)
-    c2.wait_recv()
-    c3 = send(z0_half(1 - low, -side), z0_half(1 - low, -side), cross)
-    sib.append(to_sibling(z0(-side)))
+    complete0(0)
     back1(0)
     back1(1)
-    c3.wait_recv()
-    c4 = send(z0_half(low, 2), z0_half(low, 2), pair)
-    for copy in e1:
-        copy.wait_recv()
-    sib.append(to_sibling(y1(2)))
-    for copy in e2:
-        copy.wait_recv()
-    sib.append(to_sibling(x2(2)))
+    complete(-1)
     back1(2)
+    complete0(-1)
     back1(3)
-    c4.wait_recv()
-    sib.append(to_sibling(z0(2)))
+    complete(-3)
+    complete0(-3)
     finish()
-    for copy in sib:
-        copy.wait_recv()
+    complete(-2)
+    complete0(-2)
+    arrived(sib)
     for copy in sent:
         copy.wait_send()
 
 
+def store(restored_ref, coarse_ref, restored_out, coarse_out, sem):
+    copies = [
+        pltpu.make_async_copy(coarse_ref.at[p], coarse_out.at[p], sem.at[p]) for p in range(12)
+    ] + [
+        pltpu.make_async_copy(restored_ref.at[NZ * v:NZ * v + NZ], restored_out.at[NZ * v:NZ * v + NZ], sem.at[12 + v])
+        for v in range(VARS)
+    ]
+    for copy in copies:
+        copy.start()
+    for copy in copies:
+        copy.wait()
+
+
 def body(field, masks):
-    flags = masks.astype(F32)
-    level1 = jnp.pad(jnp.repeat(flags[0], 16, 2), ((1, 0), (0, 0), (0, 64)), constant_values=1.0)
-    level2 = jnp.pad(jnp.repeat(flags[1], 8, 2), ((1, 0), (0, 0), (0, 96)), constant_values=1.0)
-    mk = jnp.stack([level1, level2]).transpose(0, 2, 1, 3)
+    mk = pltpu.with_memory_space_constraint(masks.transpose(0, 2, 3, 1), pltpu.HBM)
+    field = pltpu.with_memory_space_constraint(field.reshape(PLANES, ROWS, COLS), pltpu.HBM)
     anywhere = pl.BlockSpec(memory_space=pl.ANY)
+    in_hbm = pl.BlockSpec(memory_space=pltpu.HBM)
     in_vmem = pl.BlockSpec(memory_space=pltpu.VMEM)
     restored, coarse = pl.pallas_call(
         kernel,
@@ -518,17 +526,18 @@
             jax.ShapeDtypeStruct((PLANES, ROWS, COLS), F32),
             jax.ShapeDtypeStruct((12, 4, 4, 16, 512), F32),
         ),
-        in_specs=[anywhere, in_vmem, anywhere],
+        in_specs=[in_hbm, in_hbm],
         out_specs=(in_vmem, in_vmem),
         scratch_shapes=[
             pltpu.VMEM((PLANES, ROWS, COLS), F32),
+            pltpu.VMEM((2, 2, 4, 7), jnp.int32),
             pltpu.VMEM((512, 256), BF16),
             pltpu.VMEM((PLANES, 80, 128), F32),
             pltpu.VMEM((4, ROWS, 128), F32),
             pltpu.VMEM((4, ROWS, 128), F32),
             pltpu.VMEM((4, 80, 128), F32),
             pltpu.VMEM((4, 80, 128), F32),
-            pltpu.VMEM((8, 2, 2, 8, 128), F32),
+            pltpu.VMEM((8, 2, 2, 4, 7), jnp.int32),
             pltpu.VMEM((CLASS * 80, 512), BF16),
             pltpu.VMEM((PLANES, 2, 88, 128), F32),
             pltpu.VMEM((PLANES, 2, 40, 256), F32),
@@ -542,15 +551,27 @@
             pltpu.VMEM((3, 6, 16, 128), F32),
             pltpu.VMEM((CLASS * 64, 512), BF16),
             pltpu.VMEM((PLANES, 64, 128), F32),
-            pltpu.SemaphoreType.DMA((2,)),
+            pltpu.VMEM((2, 4, 8, 128), F32),
+            pltpu.SemaphoreType.DMA((VARS + 1,)),
             pltpu.SemaphoreType.DMA((MESSAGES,)),
             pltpu.SemaphoreType.DMA((MESSAGES,)),
         ],
         compiler_params=pltpu.CompilerParams(
-            collective_id=0, has_side_effects=True, vmem_limit_bytes=48 * 1024 * 1024
+            collective_id=0, has_side_effects=True, vmem_limit_bytes=VMEM_LIMIT
         ),
         cost_estimate=pl.CostEstimate(flops=2_000_000_000, bytes_accessed=10_000_000, transcendentals=0),
-    )(field.reshape(PLANES, ROWS, COLS), mk, jnp.asarray(lane_filters()))
+    )(field, mk)
+    restored, coarse = pl.pallas_call(
+        store,
+        out_shape=(
+            jax.ShapeDtypeStruct(restored.shape, F32),
+            jax.ShapeDtypeStruct(coarse.shape, F32),
+        ),
+        in_specs=[anywhere, anywhere],
+        out_specs=(in_hbm, in_hbm),
+        scratch_shapes=[pltpu.SemaphoreType.DMA((12 + VARS,))],
+        compiler_params=pltpu.CompilerParams(vmem_limit_bytes=1024 * 1024),
+    )(restored, coarse)
     return restored.reshape(VARS, NZ, ROWS, COLS), coarse.reshape(VARS, 4, 256, 512)
 
 

time: 71.2 us -> 58.4 us (0.82)
  local copies, waits for them, and re-layouts: 10.2 us -> 0 us
  Pallas kernels: 59.3 us -> 57.7 us
    unnamed x6 -> x0, local copies, waits for them, and re-layouts: 9.69 us -> none
    pallas_call x1, Pallas kernels: 59.3 us -> 54.4 us  [body(): pl.pallas_call(kernel, out_shape=(jax.ShapeDtypeStruct((PLANES, ROWS, COL...]
    pallas_call x0 -> x1, Pallas kernels: none -> 3.25 us  [body(): pl.pallas_call(store, out_shape=(jax.ShapeDtypeStruct(restored.shape, F32...]
where the time goes in v2:
time: 58.4 us; the launch traced here: 58.3 us
  Pallas kernels  57.7 us (99%)
  between operations  0.64 us (1%)
    pallas_call x1, Pallas kernels, body(): pl.pallas_call(kernel, out_shape=(jax.ShapeDtypeStruct((PLANES, ROWS, COL...  54.4 us
    pallas_call x1, Pallas kernels, body(): pl.pallas_call(store, out_shape=(jax.ShapeDtypeStruct(restored.shape, F32...  3.25 us

profile of v2, /device:TPU:1, one launch (start us, length us, event | category | flops | bytes accessed | tf_op | source)
XLA Modules:
  0.0 58.3 jit_solution(18437930157236588071)
XLA Ops:
  0.6 54.4 %shard_map.41 = (f32[48,64,128]{2,1,0:T(8,128)S(1)}, f32[12,4,4,16,512]{4,3,2,1,0:T(8,128)S(1)}) custom-call(f32[48,64,128]{2,1,0:T(8,128)} %bitcast.5, s32[2,2,4,7]{3,2,1,0:T(4,128)} %bitcast.7), custom_call_target="tpu_custom_call" | custom-call | flops 2000000000 | bytes 10000000 | tf_op jit(solution)/shard_map/pallas_call | solution.py:523
  55.1 3.3 %shard_map.42 = (f32[48,64,128]{2,1,0:T(8,128)}, f32[12,4,4,16,512]{4,3,2,1,0:T(8,128)}) custom-call(f32[48,64,128]{2,1,0:T(8,128)S(1)} %get-tuple-element.6.restored_ref, f32[12,4,4,16,512]{4,3,2,1,0:T(8,128)S(1)} %get-tuple-element.7.coarse_ref), custom_call_target="tpu_custom_call" | custom-call | tf_op jit(solution)/shard_map/pallas_call | solution.py:564

commit v3 on v2

--- a/solution.py
+++ b/solution.py
@@ -1,3 +1,5 @@
+import math
+
 import jax
 import jax.numpy as jnp
 from jax import lax
@@ -11,7 +13,7 @@
 VARS, NZ, ROWS, COLS = 3, 16, 64, 128
 PLANES = VARS * NZ
 CLASS = 12
-MESSAGES = 128
+BATCHES = 32
 VMEM_LIMIT = 32 * 1024 * 1024
 
 
@@ -83,9 +85,9 @@
 
 
 def kernel(
-    field_ref, masks_ref, restored_ref, g_ref,
+    field_ref, masks_ref, zr_ref, g_ref,
     x_ref, mk_ref, w_ref, t_ref, rp_ref, lp_ref, hl_ref, hr_ref, nk_ref, lhs_ref, y_ref, c_ref, s1_ref, s1l_ref, c2_ref,
-    u_ref, m1_ref, m2_ref, own_ref, parts_ref, lhsi_ref, zr_ref, j_ref, load_sem, send_sem, recv_sem,
+    u_ref, m1_ref, m2_ref, own_ref, parts_ref, lhsi_ref, j_ref, load_sem, send_sem, recv_sem,
 ):
     gx = lax.axis_index("gx")
     gy = lax.axis_index("gy")
@@ -110,12 +112,16 @@
     def along_y(k):
         return (((yy + k) % 4) * 4 + xx, gy)
 
+    def in_plane(ky, kx):
+        return (((yy + ky) % 4) * 4 + (xx + kx) % 4, gy)
+
     def along_z(k):
         return (gx, (gy + 2 * side * k + 16) % 16)
 
     greeted = around + [(gx, flip1), (gx, flip2), (gx, flip3)]
     greeted += [along_x(k) for k in (1, 2, 3)] + [along_y(k) for k in (1, 2, 3)]
     greeted += [along_z(k) for k in (1, 2, -2, 3)]
+    greeted += [in_plane(ky, kx) for ky in (1, 2, 3) for kx in (1, 2, 3)]
 
     loads = [
         pltpu.make_async_copy(field_ref.at[NZ * v:NZ * v + NZ], x_ref.at[NZ * v:NZ * v + NZ], load_sem.at[v])
@@ -129,17 +135,38 @@
         pl.semaphore_signal(barrier, inc=1, device_id=device, device_id_type=MESH)
 
     write_filters(w_ref)
-    sent = []
-
-    def send(src, dst, device):
-        i = len(sent)
-        copy = pltpu.make_async_remote_copy(
-            src_ref=src, dst_ref=dst, send_sem=send_sem.at[i], recv_sem=recv_sem.at[i],
-            device_id=device, device_id_type=MESH,
-        )
-        copy.start()
-        sent.append(copy)
-        return copy
+    batches = []
+
+    class Batch:
+        def __init__(self, sized=None):
+            self.at, self.tiles, self.sized = len(batches), 0, sized
+            batches.append(self)
+
+        def send(self, src, dst, device):
+            pltpu.make_async_remote_copy(
+                src_ref=src, dst_ref=dst, send_sem=send_sem.at[self.at], recv_sem=recv_sem.at[self.at],
+                device_id=device, device_id_type=MESH,
+            ).start()
+            if self.sized is None:
+                self.tiles += math.prod(src.shape) // 1024
+
+        def wait(self, sem):
+            size = self.sized
+            if size is None and self.tiles == 768:
+                size = g_ref.at[0:6]
+            elif size is None:
+                high = max(h for h in range(1, 9) if self.tiles % h == 0)
+                size = x_ref.at[0:self.tiles // high, 0:8 * high]
+            pltpu.make_async_copy(size, size, sem.at[self.at]).wait()
+
+        def arrived(self):
+            self.wait(recv_sem)
+
+    def batch(*copies):
+        out = Batch()
+        for copy in copies:
+            out.send(*copy)
+        return out
 
     lane = lax.broadcasted_iota(jnp.int32, (1, 128), 1)
 
@@ -173,29 +200,29 @@
     def send_halo(q, n):
         p = pl.ds(q * CLASS, n * CLASS)
         c = pl.ds(q, n)
-        return [
-            send(rp_ref.at[c], hl_ref.at[c, 8:72], (gx, right)),
-            send(lp_ref.at[c], hr_ref.at[c, 8:72], (gx, left)),
-            send(t_ref.at[p, 64:72], t_ref.at[p, 0:8], (down, gy)),
-            send(t_ref.at[p, 8:16], t_ref.at[p, 72:80], (up, gy)),
-            send(rp_ref.at[c, 56:64], hl_ref.at[c, 0:8], (down, right)),
-            send(rp_ref.at[c, 0:8], hl_ref.at[c, 72:80], (up, right)),
-            send(lp_ref.at[c, 56:64], hr_ref.at[c, 0:8], (down, left)),
-            send(lp_ref.at[c, 0:8], hr_ref.at[c, 72:80], (up, left)),
-        ]
+        return batch(
+            (rp_ref.at[c], hl_ref.at[c, 8:72], (gx, right)),
+            (lp_ref.at[c], hr_ref.at[c, 8:72], (gx, left)),
+            (t_ref.at[p, 64:72], t_ref.at[p, 0:8], (down, gy)),
+            (t_ref.at[p, 8:16], t_ref.at[p, 72:80], (up, gy)),
+            (rp_ref.at[c, 56:64], hl_ref.at[c, 0:8], (down, right)),
+            (rp_ref.at[c, 0:8], hl_ref.at[c, 72:80], (up, right)),
+            (lp_ref.at[c, 56:64], hr_ref.at[c, 0:8], (down, left)),
+            (lp_ref.at[c, 0:8], hr_ref.at[c, 72:80], (up, left)),
+        )
 
     pack(0)
     pl.semaphore_wait(barrier, len(greeted))
     halo0 = send_halo(0, 1)
     loads[VARS].wait()
-    masks_in = [send(mk_ref, nk_ref.at[n], device) for n, device in enumerate(around)]
     for q in (1, 2, 3):
         pack(q)
     halo1 = send_halo(1, 3)
+    masks_in = Batch(nk_ref)
+    for n, device in enumerate(around):
+        masks_in.send(mk_ref, nk_ref.at[n], device)
 
     def expand_masks():
-        for copy in masks_in:
-            copy.wait_recv()
         below, above, from_right, from_left, below_right, below_left, above_right, above_left = (
             nk_ref.at[n] for n in range(8)
         )
@@ -362,17 +389,6 @@
 
         lax.fori_loop(0, 3, multiply, None)
 
-    def finish():
-        for var in range(VARS):
-            slots = plane_slots(var)
-            for odd in range(2):
-                for tile in range(4):
-                    rows = slice(32 * odd + 8 * tile, 32 * odd + 8 * tile + 8)
-                    smooth, middle, fine = ([zr_ref[p, rows, :] for p in part] for part in slots)
-                    out = inverse_planes(inverse_planes(smooth, middle), fine)
-                    for k in range(NZ):
-                        restored_ref[var * NZ + k, pl.ds(16 * tile + odd, 8, stride=2), :] = out[k]
-
     def lanes_of(block):
         return pl.ds(pl.multiple_of(128 * ((block + 4) % 4), 128), 128)
 
@@ -390,27 +406,21 @@
         return g_ref.at[p2, (yy + ky + 4) % 4, (xx + kx + 4) % 4]
 
     def spread(view, axis):
-        return [send(view, view, axis(k)) for k in order]
+        return batch(*((view, view, axis(k)) for k in order))
 
     def ship0(ky):
         whole = strip0(ky, 0)
         half = strip0(ky, 0, base + low)
-        return send(whole, whole, cross), send(half, half, along_z(3))
+        return batch((whole, whole, cross), (half, half, along_z(3)))
 
     def relay0(ky, came):
-        came[0].wait_recv()
+        came.arrived()
         whole = strip0(ky, side)
-        first = send(whole, whole, pair)
-        came[1].wait_recv()
         half = strip0(ky, 2, base + 1 - low)
-        return first, send(half, half, pair)
-
-    def to_sibling(ref):
-        return send(ref, ref, sibling)
-
-    def arrived(copies):
-        for copy in copies:
-            copy.wait_recv()
+        return batch((whole, whole, pair), (half, half, pair))
+
+    def arrived(came):
+        came.arrived()
 
     arrived(halo0)
     sides_and_halves(0)
@@ -419,66 +429,70 @@
     lanes2(0)
     coarse_rows2()
     other = 1 - core
-    pre = [
-        send(own_ref.at[pl.ds(6 * other, 6)], parts_ref.at[0], (gx, flip1)),
-        send(own_ref.at[pl.ds(6 * core, 6)], parts_ref.at[1], (gx, flip2)),
-        send(own_ref.at[pl.ds(6 * other, 6)], parts_ref.at[2], (gx, flip3)),
-    ]
+    pre = batch(
+        (own_ref.at[pl.ds(6 * other, 6)], parts_ref.at[0], (gx, flip1)),
+        (own_ref.at[pl.ds(6 * core, 6)], parts_ref.at[1], (gx, flip2)),
+        (own_ref.at[pl.ds(6 * other, 6)], parts_ref.at[2], (gx, flip3)),
+    )
     lanes1(0, (1,))
-    expand_masks()
     arrived(pre)
     block = own_ref[pl.ds(base, 6)] + parts_ref[0] + parts_ref[1] + parts_ref[2]
     g_ref[pl.ds(base, 6), yy, xx, :, lanes_of(group)] = block
 
-    xs = spread(g_ref.at[p0, yy, xx, :, lanes_of(group)], along_x)
     zs = spread(g_ref.at[pl.ds(base + 2, 4), yy, xx, :, lanes_of(group)], along_z)
+    source0 = g_ref.at[p0, yy, xx, :, lanes_of(group)]
+    mine0 = g_ref.at[p0, yy, xx, :, lanes_of(group)]
+    flat0 = {}
+    for ky in (0, 1, 3, 2):
+        flat0[-ky] = batch(*((source0, mine0, in_plane(ky, kx)) for kx in (0, 1, 3, 2) if kx or ky))
+    arrived(masks_in)
+    expand_masks()
     rows1(0)
+    arrived(flat0[0])
+    s0 = {0: ship0(0)}
+    arrived(zs)
+    xs1 = [batch((strip1(0), strip1(0), along_x(k))) for k in order]
+    ys2 = [batch((strip2(0), strip2(0), along_y(k))) for k in order]
+    ys1 = {0: spread(strip1(0), along_y)}
+    xs2 = {0: spread(strip2(0), along_x)}
+    for k in order:
+        arrived(flat0[-k])
+        s0[-k] = ship0(-k)
     arrived(halo1)
     sides_and_halves(1)
     lanes1(1)
-
-    arrived(xs)
-    ys0 = spread(strip0(0, 0), along_y)
-    s0 = ship0(0)
     rows1(1)
+    for n, k in enumerate(order):
+        xs1[n].arrived()
+        ys1[-k] = spread(strip1(-k), along_y)
+        ys2[n].arrived()
+        xs2[-k] = spread(strip2(-k), along_x)
+    r0 = {0: relay0(0, s0[0])}
     lanes2(1)
-
-    arrived(zs)
-    xs1 = spread(strip1(0), along_x)
-    ys2 = spread(strip2(0), along_y)
-    ys1 = {0: spread(strip1(0), along_y)}
-    xs2 = {0: spread(strip2(0), along_x)}
     rows2(0)
     rows2(1)
-
-    s0 = {0: s0}
-    for n, k in enumerate(order):
-        ys0[n].wait_recv()
-        s0[-k] = ship0(-k)
     back2(0)
-    r0 = {0: relay0(0, s0[0])}
-    for n, k in enumerate(order):
-        xs1[n].wait_recv()
-        ys1[-k] = spread(strip1(-k), along_y)
-        ys2[n].wait_recv()
-        xs2[-k] = spread(strip2(-k), along_x)
+    r0[-1] = relay0(-1, s0[-1])
     back2(1)
     sides_and_halves(2)
     lanes1(2)
+    r0[-3] = relay0(-3, s0[-3])
     rows1(2)
-    for k in order:
-        r0[-k] = relay0(-k, s0[-k])
-    sib = []
+    r0[-2] = relay0(-2, s0[-2])
+    sib = Batch()
+
+    def to_sibling(ref):
+        sib.send(ref, ref, sibling)
 
     def complete(which):
-        arrived(ys1[which])
-        sib.append(to_sibling(g_ref.at[p1, :, (xx + which + 4) % 4]))
-        arrived(xs2[which])
-        sib.append(to_sibling(g_ref.at[p2, (yy + which + 4) % 4]))
+        ys1[which].arrived()
+        to_sibling(g_ref.at[p1, :, (xx + which + 4) % 4])
+        xs2[which].arrived()
+        to_sibling(g_ref.at[p2, (yy + which + 4) % 4])
 
     def complete0(which):
-        arrived(r0[which])
-        sib.append(to_sibling(g_ref.at[p0, (yy + which + 4) % 4]))
+        r0[which].arrived()
+        to_sibling(g_ref.at[p0, (yy + which + 4) % 4])
 
     complete(0)
     sides_and_halves(3)
@@ -493,23 +507,34 @@
     back1(3)
     complete(-3)
     complete0(-3)
-    finish()
     complete(-2)
     complete0(-2)
     arrived(sib)
-    for copy in sent:
-        copy.wait_send()
-
-
-def store(restored_ref, coarse_ref, restored_out, coarse_out, sem):
-    copies = [
-        pltpu.make_async_copy(coarse_ref.at[p], coarse_out.at[p], sem.at[p]) for p in range(12)
-    ] + [
-        pltpu.make_async_copy(restored_ref.at[NZ * v:NZ * v + NZ], restored_out.at[NZ * v:NZ * v + NZ], sem.at[12 + v])
-        for v in range(VARS)
-    ]
+    for out in batches:
+        out.wait(send_sem)
+
+
+def store(planes_ref, coarse_ref, restored_out, coarse_out, restored_ref, sem):
+    copies = [pltpu.make_async_copy(coarse_ref.at[p], coarse_out.at[p], sem.at[p]) for p in range(12)]
     for copy in copies:
         copy.start()
+    for var in range(VARS):
+        slots = plane_slots(var)
+
+        def lift(i, _, var=var, slots=slots):
+            odd, tile = i // 4, i % 4
+            rows = pl.ds(pl.multiple_of(8 * i, 8), 8)
+            smooth, middle, fine = ([planes_ref[p, rows, :] for p in part] for part in slots)
+            out = inverse_planes(inverse_planes(smooth, middle), fine)
+            for k in range(NZ):
+                restored_ref[var * NZ + k, pl.ds(16 * tile + odd, 8, stride=2), :] = out[k]
+            return _
+
+        lax.fori_loop(0, 8, lift, None)
+        planes = pl.ds(NZ * var, NZ)
+        copy = pltpu.make_async_copy(restored_ref.at[planes], restored_out.at[planes], sem.at[12 + var])
+        copy.start()
+        copies.append(copy)
     for copy in copies:
         copy.wait()
 
@@ -520,7 +545,7 @@
     anywhere = pl.BlockSpec(memory_space=pl.ANY)
     in_hbm = pl.BlockSpec(memory_space=pltpu.HBM)
     in_vmem = pl.BlockSpec(memory_space=pltpu.VMEM)
-    restored, coarse = pl.pallas_call(
+    planes, coarse = pl.pallas_call(
         kernel,
         out_shape=(
             jax.ShapeDtypeStruct((PLANES, ROWS, COLS), F32),
@@ -550,11 +575,10 @@
             pltpu.VMEM((CLASS, 16, 128), F32),
             pltpu.VMEM((3, 6, 16, 128), F32),
             pltpu.VMEM((CLASS * 64, 512), BF16),
-            pltpu.VMEM((PLANES, 64, 128), F32),
             pltpu.VMEM((2, 4, 8, 128), F32),
             pltpu.SemaphoreType.DMA((VARS + 1,)),
-            pltpu.SemaphoreType.DMA((MESSAGES,)),
-            pltpu.SemaphoreType.DMA((MESSAGES,)),
+            pltpu.SemaphoreType.DMA((BATCHES,)),
+            pltpu.SemaphoreType.DMA((BATCHES,)),
         ],
         compiler_params=pltpu.CompilerParams(
             collective_id=0, has_side_effects=True, vmem_limit_bytes=VMEM_LIMIT
@@ -564,14 +588,14 @@
     restored, coarse = pl.pallas_call(
         store,
         out_shape=(
-            jax.ShapeDtypeStruct(restored.shape, F32),
+            jax.ShapeDtypeStruct((PLANES, ROWS, COLS), F32),
             jax.ShapeDtypeStruct(coarse.shape, F32),
         ),
-        in_specs=[anywhere, anywhere],
+        in_specs=[in_vmem, anywhere],
         out_specs=(in_hbm, in_hbm),
-        scratch_shapes=[pltpu.SemaphoreType.DMA((12 + VARS,))],
-        compiler_params=pltpu.CompilerParams(vmem_limit_bytes=1024 * 1024),
-    )(restored, coarse)
+        scratch_shapes=[pltpu.VMEM((PLANES, ROWS, COLS), F32), pltpu.SemaphoreType.DMA((12 + VARS,))],
+        compiler_params=pltpu.CompilerParams(vmem_limit_bytes=4 * 1024 * 1024),
+    )(planes, coarse)
     return restored.reshape(VARS, NZ, ROWS, COLS), coarse.reshape(VARS, 4, 256, 512)
 
 

time: 58.4 us -> 54.9 us (0.940)
  Pallas kernels: 57.7 us -> 54.1 us
    pallas_call x1, Pallas kernels: 54.4 us -> 50.9 us  [body(): pl.pallas_call(kernel, out_shape=(jax.ShapeDtypeStruct((PLANES, ROWS, COL...]
where the time goes in v3:
time: 54.9 us; the launch traced here: 54.8 us
  Pallas kernels  54.1 us (99%)
  between operations  0.64 us (1%)
    pallas_call x1, Pallas kernels, body(): pl.pallas_call(kernel, out_shape=(jax.ShapeDtypeStruct((PLANES, ROWS, COL...  50.9 us
    pallas_call x1, Pallas kernels, body(): pl.pallas_call(store, out_shape=(jax.ShapeDtypeStruct((PLANES, ROWS, COLS...  3.25 us

profile of v3, /device:TPU:1, one launch (start us, length us, event | category | flops | bytes accessed | tf_op | source)
XLA Modules:
  0.0 54.8 jit_solution(2984849646871806837)
XLA Ops:
  0.6 50.9 %shard_map.41 = (f32[48,64,128]{2,1,0:T(8,128)S(1)}, f32[12,4,4,16,512]{4,3,2,1,0:T(8,128)S(1)}) custom-call(f32[48,64,128]{2,1,0:T(8,128)} %bitcast.5, s32[2,2,4,7]{3,2,1,0:T(4,128)} %bitcast.7), custom_call_target="tpu_custom_call" | custom-call | flops 2000000000 | bytes 10000000 | tf_op jit(solution)/shard_map/pallas_call | solution.py:548
  51.5 3.3 %shard_map.42 = (f32[48,64,128]{2,1,0:T(8,128)}, f32[12,4,4,16,512]{4,3,2,1,0:T(8,128)}) custom-call(f32[48,64,128]{2,1,0:T(8,128)S(1)} %get-tuple-element.6.planes_ref, f32[12,4,4,16,512]{4,3,2,1,0:T(8,128)S(1)} %get-tuple-element.7.coarse_ref), custom_call_target="tpu_custom_call" | custom-call | tf_op jit(solution)/shard_map/pallas_call | solution.py:588

commit v4 on v3

--- a/solution.py
+++ b/solution.py
@@ -448,6 +448,8 @@
     arrived(masks_in)
     expand_masks()
     rows1(0)
+    rows2(0)
+    back2(0)
     arrived(flat0[0])
     s0 = {0: ship0(0)}
     arrived(zs)
@@ -467,18 +469,7 @@
         ys1[-k] = spread(strip1(-k), along_y)
         ys2[n].arrived()
         xs2[-k] = spread(strip2(-k), along_x)
-    r0 = {0: relay0(0, s0[0])}
-    lanes2(1)
-    rows2(0)
-    rows2(1)
-    back2(0)
-    r0[-1] = relay0(-1, s0[-1])
-    back2(1)
-    sides_and_halves(2)
-    lanes1(2)
-    r0[-3] = relay0(-3, s0[-3])
-    rows1(2)
-    r0[-2] = relay0(-2, s0[-2])
+    r0 = {}
     sib = Batch()
 
     def to_sibling(ref):
@@ -494,18 +485,28 @@
         r0[which].arrived()
         to_sibling(g_ref.at[p0, (yy + which + 4) % 4])
 
+    back1(0)
+    r0[0] = relay0(0, s0[0])
+    lanes2(1)
+    rows2(1)
+    back2(1)
+    back1(1)
+    r0[-1] = relay0(-1, s0[-1])
+    sides_and_halves(2)
+    lanes1(2)
+    rows1(2)
+    r0[-3] = relay0(-3, s0[-3])
     complete(0)
+    back1(2)
     sides_and_halves(3)
     lanes1(3)
+    complete0(0)
+    complete(-1)
+    r0[-2] = relay0(-2, s0[-2])
     rows1(3)
-    complete0(0)
-    back1(0)
-    back1(1)
-    complete(-1)
-    back1(2)
     complete0(-1)
+    complete(-3)
     back1(3)
-    complete(-3)
     complete0(-3)
     complete(-2)
     complete0(-2)

time: 54.9 us -> 50.5 us (0.920)
  Pallas kernels: 54.1 us -> 49.7 us
    pallas_call x1, Pallas kernels: 50.9 us -> 46.5 us  [body(): pl.pallas_call(kernel, out_shape=(jax.ShapeDtypeStruct((PLANES, ROWS, COL...]
where the time goes in v4:
time: 50.5 us; the launch traced here: 50.3 us
  Pallas kernels  49.7 us (98%)
  between operations  0.64 us (1%)
    pallas_call x1, Pallas kernels, body(): pl.pallas_call(kernel, out_shape=(jax.ShapeDtypeStruct((PLANES, ROWS, COL...  46.5 us
    pallas_call x1, Pallas kernels, body(): pl.pallas_call(store, out_shape=(jax.ShapeDtypeStruct((PLANES, ROWS, COLS...  3.25 us

profile of v4, /device:TPU:1, one launch (start us, length us, event | category | flops | bytes accessed | tf_op | source)
XLA Modules:
  0.0 50.3 jit_solution(14703214778474607906)
XLA Ops:
  0.6 46.5 %shard_map.41 = (f32[48,64,128]{2,1,0:T(8,128)S(1)}, f32[12,4,4,16,512]{4,3,2,1,0:T(8,128)S(1)}) custom-call(f32[48,64,128]{2,1,0:T(8,128)} %bitcast.5, s32[2,2,4,7]{3,2,1,0:T(4,128)} %bitcast.7), custom_call_target="tpu_custom_call" | custom-call | flops 2000000000 | bytes 10000000 | tf_op jit(solution)/shard_map/pallas_call | solution.py:549
  47.1 3.3 %shard_map.42 = (f32[48,64,128]{2,1,0:T(8,128)}, f32[12,4,4,16,512]{4,3,2,1,0:T(8,128)}) custom-call(f32[48,64,128]{2,1,0:T(8,128)S(1)} %get-tuple-element.6.planes_ref, f32[12,4,4,16,512]{4,3,2,1,0:T(8,128)S(1)} %get-tuple-element.7.coarse_ref), custom_call_target="tpu_custom_call" | custom-call | tf_op jit(solution)/shard_map/pallas_call | solution.py:589

commit v5 on v4

--- a/solution.py
+++ b/solution.py
@@ -25,12 +25,16 @@
 
 
 FORWARD_SMOOTH = {0: 0.75, -2: -0.125, 2: -0.125, -1: 0.25, 1: 0.25}
+BOTH_SMOOTH = {}
+for _a, _v in FORWARD_SMOOTH.items():
+    for _b, _w in FORWARD_SMOOTH.items():
+        BOTH_SMOOTH[_a + 2 * _b] = BOTH_SMOOTH.get(_a + 2 * _b, 0.0) + _v * _w
 FORWARD_DETAIL = {0: -0.5, 1: 1.0, 2: -0.5}
 INVERSE_SMOOTH = {0: 1.0, -1: 0.5, 1: 0.5}
 INVERSE_DETAIL = {1: 0.75, 0: -0.25, 2: -0.25, -1: -0.125, 3: -0.125}
 
 
-def write_filters(w_ref):
+def write_filters(w_ref, wc_ref):
     row = lax.broadcasted_iota(jnp.int32, (256, 128), 0)
     col = lax.broadcasted_iota(jnp.int32, (256, 128), 1)
     cell = jnp.where(row < 136, row, jnp.where(row < 144, row - 144, 4096))
@@ -38,6 +42,8 @@
     w_ref[0:256, 128:256] = by_distance(cell - 2 * (col - 2), FORWARD_DETAIL).astype(BF16)
     w_ref[256:384, 0:128] = by_distance(col[:128] - 2 * (row[:128] - 2), INVERSE_SMOOTH).astype(BF16)
     w_ref[384:512, 0:128] = by_distance(col[:128] - 2 * (row[:128] - 2), INVERSE_DETAIL).astype(BF16)
+    away = jnp.where(col < 32, jnp.abs(cell - 4 * col), 4096)
+    wc_ref[...] = by_distance(away, {t: w for t, w in BOTH_SMOOTH.items() if t >= 0}).astype(BF16)
     row, col = row[:128], col[:128]
     ahead = row - 2 - 2 * (jnp.where(col < 64, col, col - 64) - 2)
     w_ref[256:384, 128:256] = jnp.where(
@@ -86,8 +92,8 @@
 
 def kernel(
     field_ref, masks_ref, zr_ref, g_ref,
-    x_ref, mk_ref, w_ref, t_ref, rp_ref, lp_ref, hl_ref, hr_ref, nk_ref, lhs_ref, y_ref, c_ref, s1_ref, s1l_ref, c2_ref,
-    u_ref, m1_ref, m2_ref, own_ref, parts_ref, lhsi_ref, j_ref, load_sem, send_sem, recv_sem,
+    x_ref, mk_ref, w_ref, wc_ref, yc_ref, t_ref, rp_ref, lp_ref, hl_ref, hr_ref, nk_ref, lhs_ref, y_ref, c_ref, s1_ref, s1l_ref, c2_ref,
+    u_ref, m1_ref, m2_ref, own_ref, parts_ref, pack_ref, lhsi_ref, j_ref, load_sem, send_sem, recv_sem,
 ):
     gx = lax.axis_index("gx")
     gy = lax.axis_index("gy")
@@ -134,7 +140,7 @@
     for device in greeted:
         pl.semaphore_signal(barrier, inc=1, device_id=device, device_id_type=MESH)
 
-    write_filters(w_ref)
+    write_filters(w_ref, wc_ref)
     batches = []
 
     class Batch:
@@ -198,13 +204,22 @@
         lp_ref[q] = leftward
 
     def send_halo(q, n):
-        p = pl.ds(q * CLASS, n * CLASS)
         c = pl.ds(q, n)
+        full = pl.ds(q * CLASS, CLASS)
+        fine = pl.ds((q + 1) * CLASS, (n - 1) * CLASS)
+        rows = [
+            (t_ref.at[full, 64:72], t_ref.at[full, 0:8], (down, gy)),
+            (t_ref.at[full, 8:16], t_ref.at[full, 72:80], (up, gy)),
+        ]
+        if n > 1:
+            rows += [
+                (t_ref.at[fine, 68:72], t_ref.at[fine, 4:8], (down, gy)),
+                (t_ref.at[fine, 8:12], t_ref.at[fine, 72:76], (up, gy)),
+            ]
         return batch(
+            *rows,
             (rp_ref.at[c], hl_ref.at[c, 8:72], (gx, right)),
             (lp_ref.at[c], hr_ref.at[c, 8:72], (gx, left)),
-            (t_ref.at[p, 64:72], t_ref.at[p, 0:8], (down, gy)),
-            (t_ref.at[p, 8:16], t_ref.at[p, 72:80], (up, gy)),
             (rp_ref.at[c, 56:64], hl_ref.at[c, 0:8], (down, right)),
             (rp_ref.at[c, 0:8], hl_ref.at[c, 72:80], (up, right)),
             (lp_ref.at[c, 56:64], hr_ref.at[c, 0:8], (down, left)),
@@ -283,30 +298,26 @@
 
         lax.fori_loop(0, 3, step, None)
 
-    def smooth_rows1(q):
-        def one(p):
-            even0, even1, even2 = (y_ref[p, 0, pl.ds(s, 40, stride=2), :] for s in (0, 2, 4))
-            odd0, odd1 = (y_ref[p, 0, pl.ds(s, 40, stride=2), :] for s in (1, 3))
-            detail = odd1 - 0.5 * (even1 + even2)
-            before = odd0 - 0.5 * (even0 + even1)
-            s1_ref[p] = even1 + 0.25 * (before + detail)
+    def coarse_part():
+        both = jnp.concatenate([wc_ref[...], wc_ref[...]], 0)
 
         def step(i, _):
+            rows = pl.ds(pl.multiple_of(i * 320, 320), 320)
+            yc_ref[pl.ds(4 * i, 4)] = jnp.dot(lhs_ref[rows, :], both, preferred_element_type=F32).reshape(4, 80, 128)
+            return _
+
+        lax.fori_loop(0, 3, step, None)
+
+        def lines(i, _):
             for n in range(4):
-                one(q * CLASS + 4 * i + n)
-            return _
-
-        lax.fori_loop(0, CLASS // 4, step, None)
-
-    def coarse_rows2():
-        for p in range(CLASS):
-            even0, even1, even2 = (s1l_ref[p, pl.ds(s, 16, stride=2), :] for s in (1, 3, 5))
-            odd0, odd1 = (s1l_ref[p, pl.ds(s, 16, stride=2), :] for s in (2, 4))
-            detail = odd1 - 0.5 * (even1 + even2)
-            before = odd0 - 0.5 * (even0 + even1)
-            smooth = even1 + 0.25 * (before + detail)
-            local = jnp.where((lane >= 2) & (lane < 34), smooth, 0.0)
-            own_ref[p] = pltpu.roll(local, (32 * (gy % 4) + 126) % 128, 1)
+                p = 4 * i + n
+                total = BOTH_SMOOTH[0] * yc_ref[p, pl.ds(8, 16, stride=4), :]
+                for t in range(1, 7):
+                    total += BOTH_SMOOTH[t] * (yc_ref[p, pl.ds(8 - t, 16, stride=4), :] + yc_ref[p, pl.ds(8 + t, 16, stride=4), :])
+                own_ref[p] = total
+            return _
+
+        lax.fori_loop(0, 3, lines, None)
 
     def rows1(q):
         bz = 0 if q < 2 else 1
@@ -320,9 +331,9 @@
                 before = odd0 - 0.5 * (even0 + even1)
                 smooth = even1 + 0.25 * (before + detail)
                 c_ref[p, 1, 0:40, cols] = detail * m1_ref[bz, 1, :, cols]
-                if q == 1 and half == 0:
+                if q < 2 and half == 0:
                     s1_ref[p] = smooth
-                elif q > 1 or half == 1:
+                else:
                     c_ref[p, 0, 0:40, cols] = smooth * m1_ref[bz, 0, :, cols]
 
         def step(i, _):
@@ -424,21 +435,28 @@
 
     arrived(halo0)
     sides_and_halves(0)
-    lanes1(0, (0,))
-    smooth_rows1(0)
-    lanes2(0)
-    coarse_rows2()
+    coarse_part()
+    for tile in range(3):
+        packed = own_ref[4 * tile]
+        for j in range(1, 4):
+            packed += pltpu.roll(own_ref[4 * tile + j], 32 * j, 1)
+        pack_ref[tile] = packed
     other = 1 - core
     pre = batch(
-        (own_ref.at[pl.ds(6 * other, 6)], parts_ref.at[0], (gx, flip1)),
-        (own_ref.at[pl.ds(6 * core, 6)], parts_ref.at[1], (gx, flip2)),
-        (own_ref.at[pl.ds(6 * other, 6)], parts_ref.at[2], (gx, flip3)),
+        (pack_ref.at[pl.ds(other, 2)], parts_ref.at[0], (gx, flip1)),
+        (pack_ref.at[pl.ds(core, 2)], parts_ref.at[1], (gx, flip2)),
+        (pack_ref.at[pl.ds(other, 2)], parts_ref.at[2], (gx, flip3)),
     )
-    lanes1(0, (1,))
+    lanes1(0)
     arrived(pre)
-    block = own_ref[pl.ds(base, 6)] + parts_ref[0] + parts_ref[1] + parts_ref[2]
-    g_ref[pl.ds(base, 6), yy, xx, :, lanes_of(group)] = block
-
+    for i in range(6):
+        plane = base + i
+        block = pltpu.roll(own_ref[plane], 32 * (gy % 4), 1)
+        for n, partner in enumerate((flip1, flip2, flip3)):
+            place = partner % 4
+            came = pltpu.roll(parts_ref[n, plane // 4 - core], (32 * place - 32 * (plane % 4) + 128) % 128, 1)
+            block = jnp.where(lane // 32 == place, came, block)
+        g_ref[plane, yy, xx, :, lanes_of(group)] = block
     zs = spread(g_ref.at[pl.ds(base + 2, 4), yy, xx, :, lanes_of(group)], along_z)
     source0 = g_ref.at[p0, yy, xx, :, lanes_of(group)]
     mine0 = g_ref.at[p0, yy, xx, :, lanes_of(group)]
@@ -448,6 +466,7 @@
     arrived(masks_in)
     expand_masks()
     rows1(0)
+    lanes2(0)
     rows2(0)
     back2(0)
     arrived(flat0[0])
@@ -457,13 +476,14 @@
     ys2 = [batch((strip2(0), strip2(0), along_y(k))) for k in order]
     ys1 = {0: spread(strip1(0), along_y)}
     xs2 = {0: spread(strip2(0), along_x)}
-    for k in order:
-        arrived(flat0[-k])
-        s0[-k] = ship0(-k)
+    arrived(flat0[-1])
+    s0[-1] = ship0(-1)
     arrived(halo1)
     sides_and_halves(1)
     lanes1(1)
     rows1(1)
+    arrived(flat0[-3])
+    s0[-3] = ship0(-3)
     for n, k in enumerate(order):
         xs1[n].arrived()
         ys1[-k] = spread(strip1(-k), along_y)
@@ -485,6 +505,8 @@
         r0[which].arrived()
         to_sibling(g_ref.at[p0, (yy + which + 4) % 4])
 
+    arrived(flat0[-2])
+    s0[-2] = ship0(-2)
     back1(0)
     r0[0] = relay0(0, s0[0])
     lanes2(1)
@@ -558,6 +580,8 @@
             pltpu.VMEM((PLANES, ROWS, COLS), F32),
             pltpu.VMEM((2, 2, 4, 7), jnp.int32),
             pltpu.VMEM((512, 256), BF16),
+            pltpu.VMEM((256, 128), BF16),
+            pltpu.VMEM((CLASS, 80, 128), F32),
             pltpu.VMEM((PLANES, 80, 128), F32),
             pltpu.VMEM((4, ROWS, 128), F32),
             pltpu.VMEM((4, ROWS, 128), F32),
@@ -574,7 +598,8 @@
             pltpu.VMEM((2, 2, 40, 256), F32),
             pltpu.VMEM((2, 2, 24, 128), F32),
             pltpu.VMEM((CLASS, 16, 128), F32),
-            pltpu.VMEM((3, 6, 16, 128), F32),
+            pltpu.VMEM((3, 2, 16, 128), F32),
+            pltpu.VMEM((3, 16, 128), F32),
             pltpu.VMEM((CLASS * 64, 512), BF16),
             pltpu.VMEM((2, 4, 8, 128), F32),
             pltpu.SemaphoreType.DMA((VARS + 1,)),

time: 50.5 us -> 49.1 us (0.972)
  Pallas kernels: 49.7 us -> 48.4 us
    pallas_call x1, Pallas kernels: 46.5 us -> 45.1 us  [body(): pl.pallas_call(kernel, out_shape=(jax.ShapeDtypeStruct((PLANES, ROWS, COL...]
where the time goes in v5:
time: 49.1 us; the launch traced here: 49 us
  Pallas kernels  48.4 us (99%)
  between operations  0.64 us (1%)
    pallas_call x1, Pallas kernels, body(): pl.pallas_call(kernel, out_shape=(jax.ShapeDtypeStruct((PLANES, ROWS, COL...  45.1 us
    pallas_call x1, Pallas kernels, body(): pl.pallas_call(store, out_shape=(jax.ShapeDtypeStruct((PLANES, ROWS, COLS...  3.25 us

profile of v5, /device:TPU:1, one launch (start us, length us, event | category | flops | bytes accessed | tf_op | source)
XLA Modules:
  0.0 49.0 jit_solution(17961291748585848823)
XLA Ops:
  0.6 45.1 %shard_map.41 = (f32[48,64,128]{2,1,0:T(8,128)S(1)}, f32[12,4,4,16,512]{4,3,2,1,0:T(8,128)S(1)}) custom-call(f32[48,64,128]{2,1,0:T(8,128)} %bitcast.5, s32[2,2,4,7]{3,2,1,0:T(4,128)} %bitcast.7), custom_call_target="tpu_custom_call" | custom-call | flops 2000000000 | bytes 10000000 | tf_op jit(solution)/shard_map/pallas_call | solution.py:571
  45.8 3.3 %shard_map.42 = (f32[48,64,128]{2,1,0:T(8,128)}, f32[12,4,4,16,512]{4,3,2,1,0:T(8,128)}) custom-call(f32[48,64,128]{2,1,0:T(8,128)S(1)} %get-tuple-element.6.planes_ref, f32[12,4,4,16,512]{4,3,2,1,0:T(8,128)S(1)} %get-tuple-element.7.coarse_ref), custom_call_target="tpu_custom_call" | custom-call | tf_op jit(solution)/shard_map/pallas_call | solution.py:614

commit v6 on v5

--- a/solution.py
+++ b/solution.py
@@ -14,6 +14,7 @@
 PLANES = VARS * NZ
 CLASS = 12
 BATCHES = 32
+FAMILIES = 9
 VMEM_LIMIT = 32 * 1024 * 1024
 
 
@@ -142,34 +143,38 @@
 
     write_filters(w_ref, wc_ref)
     batches = []
+    families = {}
+
+    def await_tiles(sem, tiles, size=None):
+        if size is None and tiles == 768:
+            size = g_ref.at[0:6]
+        elif size is None and tiles == 576:
+            size = g_ref.at[0:9, 0:2]
+        elif size is None:
+            high = max(h for h in range(1, 9) if tiles % h == 0)
+            size = x_ref.at[0:tiles // high, 0:8 * high]
+        pltpu.make_async_copy(size, size, sem).wait()
 
     class Batch:
-        def __init__(self, sized=None):
+        def __init__(self, sized=None, family=None):
             self.at, self.tiles, self.sized = len(batches), 0, sized
             batches.append(self)
+            self.out = families.setdefault(family or self.at, [len(families), 0, sized])
 
         def send(self, src, dst, device):
             pltpu.make_async_remote_copy(
-                src_ref=src, dst_ref=dst, send_sem=send_sem.at[self.at], recv_sem=recv_sem.at[self.at],
+                src_ref=src, dst_ref=dst, send_sem=send_sem.at[self.out[0]], recv_sem=recv_sem.at[self.at],
                 device_id=device, device_id_type=MESH,
             ).start()
             if self.sized is None:
                 self.tiles += math.prod(src.shape) // 1024
-
-        def wait(self, sem):
-            size = self.sized
-            if size is None and self.tiles == 768:
-                size = g_ref.at[0:6]
-            elif size is None:
-                high = max(h for h in range(1, 9) if self.tiles % h == 0)
-                size = x_ref.at[0:self.tiles // high, 0:8 * high]
-            pltpu.make_async_copy(size, size, sem.at[self.at]).wait()
+                self.out[1] += math.prod(src.shape) // 1024
 
         def arrived(self):
-            self.wait(recv_sem)
-
-    def batch(*copies):
-        out = Batch()
+            await_tiles(recv_sem.at[self.at], self.tiles, self.sized)
+
+    def batch(*copies, family=None):
+        out = Batch(family=family)
         for copy in copies:
             out.send(*copy)
         return out
@@ -416,19 +421,19 @@
     def strip2(ky, kx=0):
         return g_ref.at[p2, (yy + ky + 4) % 4, (xx + kx + 4) % 4]
 
-    def spread(view, axis):
-        return batch(*((view, view, axis(k)) for k in order))
+    def spread(view, axis, family="last"):
+        return batch(*((view, view, axis(k)) for k in order), family=family)
 
     def ship0(ky):
         whole = strip0(ky, 0)
         half = strip0(ky, 0, base + low)
-        return batch((whole, whole, cross), (half, half, along_z(3)))
+        return batch((whole, whole, cross), (half, half, along_z(3)), family="last")
 
     def relay0(ky, came):
         came.arrived()
         whole = strip0(ky, side)
         half = strip0(ky, 2, base + 1 - low)
-        return batch((whole, whole, pair), (half, half, pair))
+        return batch((whole, whole, pair), (half, half, pair), family="last")
 
     def arrived(came):
         came.arrived()
@@ -457,12 +462,12 @@
             came = pltpu.roll(parts_ref[n, plane // 4 - core], (32 * place - 32 * (plane % 4) + 128) % 128, 1)
             block = jnp.where(lane // 32 == place, came, block)
         g_ref[plane, yy, xx, :, lanes_of(group)] = block
-    zs = spread(g_ref.at[pl.ds(base + 2, 4), yy, xx, :, lanes_of(group)], along_z)
+    zs = spread(g_ref.at[pl.ds(base + 2, 4), yy, xx, :, lanes_of(group)], along_z, None)
     source0 = g_ref.at[p0, yy, xx, :, lanes_of(group)]
     mine0 = g_ref.at[p0, yy, xx, :, lanes_of(group)]
     flat0 = {}
     for ky in (0, 1, 3, 2):
-        flat0[-ky] = batch(*((source0, mine0, in_plane(ky, kx)) for kx in (0, 1, 3, 2) if kx or ky))
+        flat0[-ky] = batch(*((source0, mine0, in_plane(ky, kx)) for kx in (0, 1, 3, 2) if kx or ky), family="flat")
     arrived(masks_in)
     expand_masks()
     rows1(0)
@@ -472,8 +477,8 @@
     arrived(flat0[0])
     s0 = {0: ship0(0)}
     arrived(zs)
-    xs1 = [batch((strip1(0), strip1(0), along_x(k))) for k in order]
-    ys2 = [batch((strip2(0), strip2(0), along_y(k))) for k in order]
+    xs1 = [batch((strip1(0), strip1(0), along_x(k)), family="middle") for k in order]
+    ys2 = [batch((strip2(0), strip2(0), along_y(k)), family="middle") for k in order]
     ys1 = {0: spread(strip1(0), along_y)}
     xs2 = {0: spread(strip2(0), along_x)}
     arrived(flat0[-1])
@@ -533,8 +538,8 @@
     complete(-2)
     complete0(-2)
     arrived(sib)
-    for out in batches:
-        out.wait(send_sem)
+    for at, tiles, size in families.values():
+        await_tiles(send_sem.at[at], tiles, size)
 
 
 def store(planes_ref, coarse_ref, restored_out, coarse_out, restored_ref, sem):
@@ -555,7 +560,7 @@
 
         lax.fori_loop(0, 8, lift, None)
         planes = pl.ds(NZ * var, NZ)
-        copy = pltpu.make_async_copy(restored_ref.at[planes], restored_out.at[planes], sem.at[12 + var])
+        copy = pltpu.make_async_copy(restored_ref.at[planes, 0:ROWS], restored_out.at[planes], sem.at[12 + var])
         copy.start()
         copies.append(copy)
     for copy in copies:
@@ -603,7 +608,7 @@
             pltpu.VMEM((CLASS * 64, 512), BF16),
             pltpu.VMEM((2, 4, 8, 128), F32),
             pltpu.SemaphoreType.DMA((VARS + 1,)),
-            pltpu.SemaphoreType.DMA((BATCHES,)),
+            pltpu.SemaphoreType.DMA((FAMILIES,)),
             pltpu.SemaphoreType.DMA((BATCHES,)),
         ],
         compiler_params=pltpu.CompilerParams(
@@ -619,8 +624,8 @@
         ),
         in_specs=[in_vmem, anywhere],
         out_specs=(in_hbm, in_hbm),
-        scratch_shapes=[pltpu.VMEM((PLANES, ROWS, COLS), F32), pltpu.SemaphoreType.DMA((12 + VARS,))],
-        compiler_params=pltpu.CompilerParams(vmem_limit_bytes=4 * 1024 * 1024),
+        scratch_shapes=[pltpu.VMEM((PLANES, ROWS + 8, COLS), F32), pltpu.SemaphoreType.DMA((12 + VARS,))],
+        compiler_params=pltpu.CompilerParams(vmem_limit_bytes=5 * 1024 * 1024),
     )(planes, coarse)
     return restored.reshape(VARS, NZ, ROWS, COLS), coarse.reshape(VARS, 4, 256, 512)
 

time: 49.1 us -> 48.9 us (level)
  no operation moved by 1% of the time
where the time goes in v6:
time: 48.9 us; the launch traced here: 48.8 us
  Pallas kernels  48.1 us (98%)
  between operations  0.64 us (1%)
    pallas_call x1, Pallas kernels, body(): pl.pallas_call(kernel, out_shape=(jax.ShapeDtypeStruct((PLANES, ROWS, COL...  44.9 us
    pallas_call x1, Pallas kernels, body(): pl.pallas_call(store, out_shape=(jax.ShapeDtypeStruct((PLANES, ROWS, COLS...  3.25 us

profile of v6, /device:TPU:1, one launch (start us, length us, event | category | flops | bytes accessed | tf_op | source)
XLA Modules:
  0.0 48.8 jit_solution(13600470065548897288)
XLA Ops:
  0.6 44.9 %shard_map.41 = (f32[48,64,128]{2,1,0:T(8,128)S(1)}, f32[12,4,4,16,512]{4,3,2,1,0:T(8,128)S(1)}) custom-call(f32[48,64,128]{2,1,0:T(8,128)} %bitcast.5, s32[2,2,4,7]{3,2,1,0:T(4,128)} %bitcast.7), custom_call_target="tpu_custom_call" | custom-call | flops 2000000000 | bytes 10000000 | tf_op jit(solution)/shard_map/pallas_call | solution.py:576
  45.5 3.3 %shard_map.42 = (f32[48,64,128]{2,1,0:T(8,128)}, f32[12,4,4,16,512]{4,3,2,1,0:T(8,128)}) custom-call(f32[48,64,128]{2,1,0:T(8,128)S(1)} %get-tuple-element.6.planes_ref, f32[12,4,4,16,512]{4,3,2,1,0:T(8,128)S(1)} %get-tuple-element.7.coarse_ref), custom_call_target="tpu_custom_call" | custom-call | tf_op jit(solution)/shard_map/pallas_call | solution.py:619

commit v7 on v6

--- a/solution.py
+++ b/solution.py
@@ -237,7 +237,6 @@
     loads[VARS].wait()
     for q in (1, 2, 3):
         pack(q)
-    halo1 = send_halo(1, 3)
     masks_in = Batch(nk_ref)
     for n, device in enumerate(around):
         masks_in.send(mk_ref, nk_ref.at[n], device)
@@ -439,6 +438,7 @@
         came.arrived()
 
     arrived(halo0)
+    halo1 = send_halo(1, 3)
     sides_and_halves(0)
     coarse_part()
     for tile in range(3):

time: 48.9 us -> 48.8 us (level)
  no operation moved by 1% of the time
where the time goes in v7:
time: 48.8 us; the launch traced here: 48.7 us
  Pallas kernels  48 us (98%)
  between operations  0.64 us (1%)
    pallas_call x1, Pallas kernels, body(): pl.pallas_call(kernel, out_shape=(jax.ShapeDtypeStruct((PLANES, ROWS, COL...  44.8 us
    pallas_call x1, Pallas kernels, body(): pl.pallas_call(store, out_shape=(jax.ShapeDtypeStruct((PLANES, ROWS, COLS...  3.25 us

profile of v7, /device:TPU:1, one launch (start us, length us, event | category | flops | bytes accessed | tf_op | source)
XLA Modules:
  0.0 48.7 jit_solution(13758707717114258763)
XLA Ops:
  0.6 44.8 %shard_map.41 = (f32[48,64,128]{2,1,0:T(8,128)S(1)}, f32[12,4,4,16,512]{4,3,2,1,0:T(8,128)S(1)}) custom-call(f32[48,64,128]{2,1,0:T(8,128)} %bitcast.5, s32[2,2,4,7]{3,2,1,0:T(4,128)} %bitcast.7), custom_call_target="tpu_custom_call" | custom-call | flops 2000000000 | bytes 10000000 | tf_op jit(solution)/shard_map/pallas_call | solution.py:576
  45.4 3.3 %shard_map.42 = (f32[48,64,128]{2,1,0:T(8,128)}, f32[12,4,4,16,512]{4,3,2,1,0:T(8,128)}) custom-call(f32[48,64,128]{2,1,0:T(8,128)S(1)} %get-tuple-element.6.planes_ref, f32[12,4,4,16,512]{4,3,2,1,0:T(8,128)S(1)} %get-tuple-element.7.coarse_ref), custom_call_target="tpu_custom_call" | custom-call | tf_op jit(solution)/shard_map/pallas_call | solution.py:619
